TPU v7x, 32 devices: a whole 2x2x4 slice. The times are simulated.
32 devices in a mesh: blk: 16 (over z, y, core), tp: 2 (over x).
Axes of the slice: x: 2, y: 2, z: 4, core: 2. Of those that a mesh axis runs over, the one named last changes fastest.
Arguments:
- encoder_in: bfloat16 [4096, 768], P('blk'), may hold values from -6 to 6
- decoder_in: bfloat16 [2048, 768], P('blk'), may hold values from -6 to 6
- lengths: int32 [16], P('blk'), may hold values from 64 to 128, as said below
- retrieved: int32 [2048, 12, 1024], P('blk', 'tp'), may hold values from 0 to 2047, as said below
- band_start: int32 [2048, 12], P('blk', 'tp'), may hold values from 0 to 8, as said below
- cotangent: bfloat16 [2048, 768], P('blk'), may hold values from -6 to 6
- enc_query: bfloat16 [768, 768], P(None, 'tp'), may hold values from -0.21875 to 0.21875
- enc_key: bfloat16 [768, 768], P(None, 'tp'), may hold values from -0.21875 to 0.21875
- enc_value: bfloat16 [768, 768], P(None, 'tp'), may hold values from -0.21875 to 0.21875
- enc_mix: bfloat16 [768, 768], P('tp'), may hold values from -1.75 to 1.75
- attn_gain: bfloat16 [768], replicated, may hold values from 0.5 to 1.5
- attn_shift: bfloat16 [768], replicated, may hold values from -1.1953125 to 1.1953125
- enc_up: bfloat16 [768, 3072], P(None, 'tp'), may hold values from -0.21875 to 0.21875
- enc_down: bfloat16 [3072, 768], P('tp'), may hold values from -0.109375 to 0.109375
- ffn_gain: bfloat16 [768], replicated, may hold values from 0.5 to 1.5
- ffn_shift: bfloat16 [768], replicated, may hold values from -1.1953125 to 1.1953125
- self_query: bfloat16 [768, 768], P(None, 'tp'), may hold values from -0.21875 to 0.21875
- self_key: bfloat16 [768, 768], P(None, 'tp'), may hold values from -0.21875 to 0.21875
- self_value: bfloat16 [768, 768], P(None, 'tp'), may hold values from -0.21875 to 0.21875
- self_mix: bfloat16 [768, 768], P('tp'), may hold values from -1.25 to 1.25
- self_gain: bfloat16 [768], replicated, may hold values from 0.5 to 1.5
- self_shift: bfloat16 [768], replicated, may hold values from -1.1953125 to 1.1953125
- cross_query: bfloat16 [768, 768], P(None, 'tp'), may hold values from -0.21875 to 0.21875
- cross_key: bfloat16 [768, 768], P(None, 'tp'), may hold values from -0.21875 to 0.21875
- cross_value: bfloat16 [768, 768], P(None, 'tp'), may hold values from -0.21875 to 0.21875
- cross_mix: bfloat16 [768, 768], P('tp'), may hold values from -3.5 to 3.5
- cross_gain: bfloat16 [768], replicated, may hold values from 0.5 to 1.5
- cross_shift: bfloat16 [768], replicated, may hold values from -1.1953125 to 1.1953125
- dec_up: bfloat16 [768, 3072], P(None, 'tp'), may hold values from -0.21875 to 0.21875
- dec_down: bfloat16 [3072, 768], P('tp'), may hold values from -0.109375 to 0.109375
- last_gain: bfloat16 [768], replicated, may hold values from 0.5 to 1.5
- last_shift: bfloat16 [768], replicated, may hold values from -1.1953125 to 1.1953125
Outputs:
- encoded: float32 [4096, 768], P('blk')
- decoded: float32 [2048, 768], P('blk')
- grad_encoder_in: float32 [4096, 768], P('blk')
- grad_decoder_in: float32 [2048, 768], P('blk')
- grad_enc_query: float32 [768, 768], P('blk', 'tp')
- grad_enc_key: float32 [768, 768], P('blk', 'tp')
- grad_enc_value: float32 [768, 768], P('blk', 'tp')
- grad_enc_mix: float32 [768, 768], P('tp', 'blk')
- grad_attn_gain: float32 [768], P('blk')
- grad_attn_shift: float32 [768], P('blk')
- grad_enc_up: float32 [768, 3072], P('blk', 'tp')
- grad_enc_down: float32 [3072, 768], P('tp', 'blk')
- grad_ffn_gain: float32 [768], P('blk')
- grad_ffn_shift: float32 [768], P('blk')
- grad_self_query: float32 [768, 768], P('blk', 'tp')
- grad_self_key: float32 [768, 768], P('blk', 'tp')
- grad_self_value: float32 [768, 768], P('blk', 'tp')
- grad_self_mix: float32 [768, 768], P('tp', 'blk')
- grad_self_gain: float32 [768], P('blk')
- grad_self_shift: float32 [768], P('blk')
- grad_cross_query: float32 [768, 768], P('blk', 'tp')
- grad_cross_key: float32 [768, 768], P('blk', 'tp')
- grad_cross_value: float32 [768, 768], P('blk', 'tp')
- grad_cross_mix: float32 [768, 768], P('tp', 'blk')
- grad_cross_gain: float32 [768], P('blk')
- grad_cross_shift: float32 [768], P('blk')
- grad_dec_up: float32 [768, 3072], P('blk', 'tp')
- grad_dec_down: float32 [3072, 768], P('tp', 'blk')
- grad_last_gain: float32 [768], P('blk')
- grad_last_shift: float32 [768], P('blk')
Inputs may be any that keep to these rules, and one draw needn't show every extreme that they name: `lengths`: the largest length is 128 and the smallest 64 in every draw. `retrieved`: for each decoder row and head, 1024 distinct offsets in ascending order into its band of 8 consecutive groups of 256 rows: exactly one of each pair 2i, 2i + 1. `band_start`: bands starting at group 0 and at group 16 - 8 occur in every draw.
All inputs are finite; a program needn't handle non-finite values.
Results may differ from a plain program's by a relative error of at most 0.028.
Values may be sent and summed in bfloat16 or wider, within the bound.
No kernel may reach another device: no remote copies, remote signals or barrier semaphores. Data moves between devices by JAX's collectives and lax.ppermute only.
A program may use at most 704 MiB of HBM per device.

v0:
```python
import jax
import jax.numpy as jnp
from jax import lax
from jax.sharding import PartitionSpec as P

HD = 64


NEG_FILL = -1e30
EPS_NORM = 1e-05


def head_sum(partial_value):
    return lax.psum(partial_value, "tp")


def matmul(inputs, matrix):
    return jnp.dot(inputs, matrix, preferred_element_type=jnp.float32)


def outer(inputs, grads):
    return lax.dot_general(
        inputs, grads, (((0,), (0,)), ((), ())), preferred_element_type=jnp.float32
    )


def backward_of(grads, matrix):
    return lax.dot_general(
        grads, matrix, (((1,), (1,)), ((), ())), preferred_element_type=jnp.float32
    )


def layer_norm(inputs, norm_gain, norm_shift):
    center = inputs - jnp.mean(inputs, -1, keepdims=True)
    spread = jnp.mean(center * center, -1, keepdims=True)
    return center * lax.rsqrt(spread + EPS_NORM) * norm_gain + norm_shift


def norm_back(inputs, norm_gain, norm_shift, upstream):
    outputs, pullback = jax.vjp(layer_norm, inputs, norm_gain, norm_shift)
    return pullback(upstream)


def exact_gelu(tensor):
    return jax.nn.gelu(tensor, approximate=False)


def split_heads(tensor):
    return tensor.reshape(tensor.shape[0], tensor.shape[1] // HD, HD)


def local_probs(queries, key_rows, allowed):
    scores = (
        jnp.einsum("qhd,khd->hqk", queries, key_rows, preferred_element_type=jnp.float32) * 0.125
    )
    return jax.nn.softmax(jnp.where(allowed[None], scores, NEG_FILL), axis=-1)


def attend_fwd(low_in, query_mat, key_mat, value_mat, allowed):
    queries = split_heads(matmul(low_in, query_mat).astype(jnp.bfloat16))
    key_rows = split_heads(matmul(low_in, key_mat).astype(jnp.bfloat16))
    value_rows = split_heads(matmul(low_in, value_mat).astype(jnp.bfloat16))
    weights = local_probs(queries, key_rows, allowed)
    mixed = jnp.einsum(
        "hqk,khd->qhd", weights.astype(jnp.bfloat16), value_rows, preferred_element_type=jnp.float32
    )
    mixed = mixed.reshape(low_in.shape[0], -1).astype(jnp.bfloat16)
    return ((queries, key_rows, value_rows), mixed)


def attend_back(low_in, query_mat, key_mat, value_mat, saved_qkv, allowed, grad_mixed):
    queries, key_rows, value_rows = saved_qkv
    row_count = low_in.shape[0]
    weights = local_probs(queries, key_rows, allowed)
    grad_heads = split_heads(grad_mixed)
    grad_value = jnp.einsum(
        "hqk,qhd->khd", weights.astype(jnp.bfloat16), grad_heads, preferred_element_type=jnp.float32
    )
    grad_weights = jnp.einsum(
        "qhd,khd->hqk", grad_heads, value_rows, preferred_element_type=jnp.float32
    )
    grad_scores = weights * (grad_weights - jnp.sum(weights * grad_weights, -1, keepdims=True))
    grad_scores = grad_scores.astype(jnp.bfloat16)
    grad_query = (
        jnp.einsum("hqk,khd->qhd", grad_scores, key_rows, preferred_element_type=jnp.float32)
        * 0.125
    )
    grad_key = (
        jnp.einsum("hqk,qhd->khd", grad_scores, queries, preferred_element_type=jnp.float32) * 0.125
    )
    query_grad = grad_query.reshape(row_count, -1).astype(jnp.bfloat16)
    key_grad = grad_key.reshape(row_count, -1).astype(jnp.bfloat16)
    value_grad = grad_value.reshape(row_count, -1).astype(jnp.bfloat16)
    partial_value = (
        backward_of(query_grad, query_mat)
        + backward_of(key_grad, key_mat)
        + backward_of(value_grad, value_mat)
    )
    return (
        (outer(low_in, query_grad), outer(low_in, key_grad), outer(low_in, value_grad)),
        partial_value,
    )


def feed_fwd(low_in, up_mat, down_mat):
    hidden = matmul(low_in, up_mat)
    active = exact_gelu(hidden).astype(jnp.bfloat16)
    return (hidden, active, head_sum(matmul(active, down_mat)))


def feed_back(low_in, hidden, active, up_mat, down_mat, grad_branch):
    branch_low = grad_branch.astype(jnp.bfloat16)
    grad_active = backward_of(branch_low, down_mat)
    grad_down = outer(active, branch_low)
    outputs, pullback = jax.vjp(exact_gelu, hidden)
    hidden_grad = pullback(grad_active)[0].astype(jnp.bfloat16)
    return (outer(low_in, hidden_grad), grad_down, head_sum(backward_of(hidden_grad, up_mat)))


def on_device(
    encoder_in,
    decoder_in,
    lengths,
    retrieved,
    band_start,
    cotangent,
    enc_query,
    enc_key,
    enc_value,
    enc_mix,
    attn_gain,
    attn_shift,
    enc_up,
    enc_down,
    ffn_gain,
    ffn_shift,
    self_query,
    self_key,
    self_value,
    self_mix,
    self_gain,
    self_shift,
    cross_query,
    cross_key,
    cross_value,
    cross_mix,
    cross_gain,
    cross_shift,
    dec_up,
    dec_down,
    last_gain,
    last_shift,
):
    group_rows = encoder_in.shape[0]
    slot_rows = decoder_in.shape[0]
    head_count = cross_query.shape[1] // HD
    picked_count = retrieved.shape[2]
    band_width = 2 * picked_count // group_rows
    attn_gain_f = attn_gain.astype(jnp.float32)
    attn_shift_f = attn_shift.astype(jnp.float32)
    ffn_gain_f = ffn_gain.astype(jnp.float32)
    ffn_shift_f = ffn_shift.astype(jnp.float32)
    self_gain_f = self_gain.astype(jnp.float32)
    self_shift_f = self_shift.astype(jnp.float32)
    cross_gain_f = cross_gain.astype(jnp.float32)
    cross_shift_f = cross_shift.astype(jnp.float32)
    last_gain_f = last_gain.astype(jnp.float32)
    last_shift_f = last_shift.astype(jnp.float32)
    enc_float = encoder_in.astype(jnp.float32)
    full_mask = jnp.ones((group_rows, group_rows), jnp.bool_)
    enc_kept, enc_mixed = attend_fwd(encoder_in, enc_query, enc_key, enc_value, full_mask)
    attn_sum = enc_float + head_sum(matmul(enc_mixed, enc_mix))
    first_enc = layer_norm(attn_sum, attn_gain_f, attn_shift_f)
    first_low = first_enc.astype(jnp.bfloat16)
    enc_hidden, enc_active, enc_branch = feed_fwd(first_low, enc_up, enc_down)
    ffn_sum = first_enc + enc_branch
    encoded_float = layer_norm(ffn_sum, ffn_gain_f, ffn_shift_f)
    encoded = encoded_float.astype(jnp.bfloat16)
    store_pair = jnp.stack(
        [
            matmul(encoded, cross_key).astype(jnp.bfloat16),
            matmul(encoded, cross_value).astype(jnp.bfloat16),
        ]
    )
    dec_float = decoder_in.astype(jnp.float32)
    positions = jnp.arange(slot_rows, dtype=jnp.int32)
    causal = (positions[None, :] <= positions[:, None]) & (positions[None, :] < lengths[0])
    self_kept, self_mixed = attend_fwd(decoder_in, self_query, self_key, self_value, causal)
    self_sum = dec_float + head_sum(matmul(self_mixed, self_mix))
    first_dec = layer_norm(self_sum, self_gain_f, self_shift_f)
    first_dlow = first_dec.astype(jnp.bfloat16)
    cross_q = split_heads(matmul(first_dlow, cross_query).astype(jnp.bfloat16))
    pair_picks = (retrieved - 2 * jnp.arange(picked_count, dtype=jnp.int32)).astype(jnp.bfloat16)
    pair_picks = pair_picks.reshape(slot_rows, head_count, band_width, group_rows // 2)
    band_slots = jnp.arange(band_width, dtype=jnp.int32)
    parity = jnp.arange(2, dtype=jnp.float32)

    def block_mask(piece_rows):
        count = piece_rows // group_rows
        group_ids = jnp.arange(count, dtype=jnp.int32)
        relative = group_ids[None, None, :] - band_start[:, :, None]
        onehot = (relative[..., None] == band_slots).astype(jnp.bfloat16)
        in_band = (relative >= 0) & (relative < band_width)
        pick_sel = jnp.einsum(
            "shcb,shbp->shcp", onehot, pair_picks, preferred_element_type=jnp.float32
        )
        chosen = in_band[..., None, None] & (parity == pick_sel[..., None])
        return chosen.reshape(slot_rows, head_count, piece_rows)

    key_block = lax.all_gather(store_pair, "blk", axis=1, tiled=True)
    run_max = jnp.full((slot_rows, head_count), NEG_FILL, jnp.float32)
    piece_rows = key_block.shape[1]
    key_piece = split_heads(key_block[0])
    value_piece = split_heads(key_block[1])
    chosen = block_mask(piece_rows)
    scores = (
        jnp.einsum("qhd,khd->qhk", cross_q, key_piece, preferred_element_type=jnp.float32) * 0.125
    )
    new_max = jnp.maximum(run_max, jnp.max(jnp.where(chosen, scores, NEG_FILL), -1))
    exp_scores = jnp.where(chosen, jnp.exp(scores - new_max[..., None]), 0.0)
    run_sum = jnp.sum(exp_scores, -1)
    run_acc = jnp.einsum(
        "qhk,khd->qhd",
        exp_scores.astype(jnp.bfloat16),
        value_piece,
        preferred_element_type=jnp.float32,
    )
    fold_state = (new_max, run_sum, run_acc)
    run_max, run_sum, run_acc = fold_state
    cross_float = run_acc / run_sum[..., None]
    log_total = run_max + jnp.log(run_sum)
    cross_mixed = cross_float.reshape(slot_rows, -1).astype(jnp.bfloat16)
    cross_sum = first_dec + head_sum(matmul(cross_mixed, cross_mix))
    second_dec = layer_norm(cross_sum, cross_gain_f, cross_shift_f)
    second_low = second_dec.astype(jnp.bfloat16)
    dec_hidden, dec_active, dec_branch = feed_fwd(second_low, dec_up, dec_down)
    last_sum = second_dec + dec_branch
    decoded = layer_norm(last_sum, last_gain_f, last_shift_f)
    grad_last, grad_last_gain, grad_last_shift = norm_back(
        last_sum, last_gain_f, last_shift_f, cotangent.astype(jnp.float32)
    )
    grad_dec_up, grad_dec_down, dec_partial = feed_back(
        second_low, dec_hidden, dec_active, dec_up, dec_down, grad_last
    )
    grad_second = grad_last + dec_partial
    grad_cross, grad_cross_gain, grad_cross_shift = norm_back(
        cross_sum, cross_gain_f, cross_shift_f, grad_second
    )
    cross_low = grad_cross.astype(jnp.bfloat16)
    grad_cross_mix = outer(cross_mixed, cross_low)
    grad_heads = split_heads(backward_of(cross_low, cross_mix).astype(jnp.bfloat16))
    delta_rows = jnp.sum(grad_heads.astype(jnp.float32) * cross_float, -1)
    key_block = lax.all_gather(store_pair, "blk", axis=1, tiled=True)
    piece_rows = key_block.shape[1]
    key_piece = split_heads(key_block[0])
    value_piece = split_heads(key_block[1])
    chosen = block_mask(piece_rows)
    scores = (
        jnp.einsum("qhd,khd->qhk", cross_q, key_piece, preferred_element_type=jnp.float32) * 0.125
    )
    weights = jnp.where(chosen, jnp.exp(scores - log_total[..., None]), 0.0)
    value_grad = jnp.einsum(
        "qhk,qhd->khd", weights.astype(jnp.bfloat16), grad_heads, preferred_element_type=jnp.float32
    )
    grad_weights = jnp.einsum(
        "qhd,khd->qhk", grad_heads, value_piece, preferred_element_type=jnp.float32
    )
    grad_scores = (weights * (grad_weights - delta_rows[..., None])).astype(jnp.bfloat16)
    back_grad_query = (
        jnp.einsum("qhk,khd->qhd", grad_scores, key_piece, preferred_element_type=jnp.float32)
        * 0.125
    )
    key_grad = (
        jnp.einsum("qhk,qhd->khd", grad_scores, cross_q, preferred_element_type=jnp.float32) * 0.125
    )
    block_term = jnp.stack([key_grad.reshape(piece_rows, -1), value_grad.reshape(piece_rows, -1)])
    grad_query, block_term = (back_grad_query, block_term)
    grad_store = block_term
    back_result = (grad_query, grad_store)
    grad_query_all, grad_store = back_result
    store_grad = lax.psum_scatter(grad_store, "blk", scatter_dimension=1, tiled=True).astype(
        jnp.bfloat16
    )
    query_low = grad_query_all.reshape(slot_rows, -1).astype(jnp.bfloat16)
    grad_cross_query = outer(first_dlow, query_low)
    grad_first = grad_cross + head_sum(backward_of(query_low, cross_query))
    grad_self, grad_self_gain, grad_self_shift = norm_back(
        self_sum, self_gain_f, self_shift_f, grad_first
    )
    self_low = grad_self.astype(jnp.bfloat16)
    grad_self_mix = outer(self_mixed, self_low)
    self_grads, self_partial = attend_back(
        decoder_in,
        self_query,
        self_key,
        self_value,
        self_kept,
        causal,
        backward_of(self_low, self_mix).astype(jnp.bfloat16),
    )
    grad_decoder_in = grad_self + head_sum(self_partial)
    grad_cross_key = outer(encoded, store_grad[0])
    grad_cross_value = outer(encoded, store_grad[1])
    grad_encoded = head_sum(
        backward_of(store_grad[0], cross_key) + backward_of(store_grad[1], cross_value)
    )
    grad_ffn, grad_ffn_gain, grad_ffn_shift = norm_back(
        ffn_sum, ffn_gain_f, ffn_shift_f, grad_encoded
    )
    grad_enc_up, grad_enc_down, enc_partial = feed_back(
        first_low, enc_hidden, enc_active, enc_up, enc_down, grad_ffn
    )
    grad_first_enc = grad_ffn + enc_partial
    grad_attn, grad_attn_gain, grad_attn_shift = norm_back(
        attn_sum, attn_gain_f, attn_shift_f, grad_first_enc
    )
    attn_low = grad_attn.astype(jnp.bfloat16)
    grad_enc_mix = outer(enc_mixed, attn_low)
    enc_grads, enc_partial_in = attend_back(
        encoder_in,
        enc_query,
        enc_key,
        enc_value,
        enc_kept,
        full_mask,
        backward_of(attn_low, enc_mix).astype(jnp.bfloat16),
    )
    grad_encoder_in = grad_attn + head_sum(enc_partial_in)
    reduced = (
        lax.psum_scatter(enc_grads[0], "blk", scatter_dimension=0, tiled=True),
        lax.psum_scatter(enc_grads[1], "blk", scatter_dimension=0, tiled=True),
        lax.psum_scatter(enc_grads[2], "blk", scatter_dimension=0, tiled=True),
        lax.psum_scatter(grad_enc_mix, "blk", scatter_dimension=1, tiled=True),
        lax.psum_scatter(grad_attn_gain, "blk", scatter_dimension=0, tiled=True),
        lax.psum_scatter(grad_attn_shift, "blk", scatter_dimension=0, tiled=True),
        lax.psum_scatter(grad_enc_up, "blk", scatter_dimension=0, tiled=True),
        lax.psum_scatter(grad_enc_down, "blk", scatter_dimension=1, tiled=True),
        lax.psum_scatter(grad_ffn_gain, "blk", scatter_dimension=0, tiled=True),
        lax.psum_scatter(grad_ffn_shift, "blk", scatter_dimension=0, tiled=True),
        lax.psum_scatter(self_grads[0], "blk", scatter_dimension=0, tiled=True),
        lax.psum_scatter(self_grads[1], "blk", scatter_dimension=0, tiled=True),
        lax.psum_scatter(self_grads[2], "blk", scatter_dimension=0, tiled=True),
        lax.psum_scatter(grad_self_mix, "blk", scatter_dimension=1, tiled=True),
        lax.psum_scatter(grad_self_gain, "blk", scatter_dimension=0, tiled=True),
        lax.psum_scatter(grad_self_shift, "blk", scatter_dimension=0, tiled=True),
        lax.psum_scatter(grad_cross_query, "blk", scatter_dimension=0, tiled=True),
        lax.psum_scatter(grad_cross_key, "blk", scatter_dimension=0, tiled=True),
        lax.psum_scatter(grad_cross_value, "blk", scatter_dimension=0, tiled=True),
        lax.psum_scatter(grad_cross_mix, "blk", scatter_dimension=1, tiled=True),
        lax.psum_scatter(grad_cross_gain, "blk", scatter_dimension=0, tiled=True),
        lax.psum_scatter(grad_cross_shift, "blk", scatter_dimension=0, tiled=True),
        lax.psum_scatter(grad_dec_up, "blk", scatter_dimension=0, tiled=True),
        lax.psum_scatter(grad_dec_down, "blk", scatter_dimension=1, tiled=True),
        lax.psum_scatter(grad_last_gain, "blk", scatter_dimension=0, tiled=True),
        lax.psum_scatter(grad_last_shift, "blk", scatter_dimension=0, tiled=True),
    )
    return (
        encoded_float,
        decoded,
        grad_encoder_in,
        grad_decoder_in,
        reduced[0],
        reduced[1],
        reduced[2],
        reduced[3],
        reduced[4],
        reduced[5],
        reduced[6],
        reduced[7],
        reduced[8],
        reduced[9],
        reduced[10],
        reduced[11],
        reduced[12],
        reduced[13],
        reduced[14],
        reduced[15],
        reduced[16],
        reduced[17],
        reduced[18],
        reduced[19],
        reduced[20],
        reduced[21],
        reduced[22],
        reduced[23],
        reduced[24],
        reduced[25],
    )


def solution(mesh):
    in_specs = (
        P("blk", None),
        P("blk", None),
        P("blk"),
        P("blk", "tp", None),
        P("blk", "tp"),
        P("blk", None),
        P(None, "tp"),
        P(None, "tp"),
        P(None, "tp"),
        P("tp", None),
        P(),
        P(),
        P(None, "tp"),
        P("tp", None),
        P(),
        P(),
        P(None, "tp"),
        P(None, "tp"),
        P(None, "tp"),
        P("tp", None),
        P(),
        P(),
        P(None, "tp"),
        P(None, "tp"),
        P(None, "tp"),
        P("tp", None),
        P(),
        P(),
        P(None, "tp"),
        P("tp", None),
        P(),
        P(),
    )
    out_specs = (
        P("blk", None),
        P("blk", None),
        P("blk", None),
        P("blk", None),
        P("blk", "tp"),
        P("blk", "tp"),
        P("blk", "tp"),
        P("tp", "blk"),
        P("blk"),
        P("blk"),
        P("blk", "tp"),
        P("tp", "blk"),
        P("blk"),
        P("blk"),
        P("blk", "tp"),
        P("blk", "tp"),
        P("blk", "tp"),
        P("tp", "blk"),
        P("blk"),
        P("blk"),
        P("blk", "tp"),
        P("blk", "tp"),
        P("blk", "tp"),
        P("tp", "blk"),
        P("blk"),
        P("blk"),
        P("blk", "tp"),
        P("tp", "blk"),
        P("blk"),
        P("blk"),
    )
    return jax.shard_map(
        on_device, mesh=mesh, in_specs=in_specs, out_specs=out_specs, check_vma=False
    )
```

profile of v0, /device:TPU:0, one launch (start us, length us, event | category | flops | bytes accessed | tf_op | source)
XLA Modules:
  0.0 1726.8 jit_solution(8874201718290150988)
XLA Ops:
  30.3 24.6 %all-reduce.23.cloned.1.call-done = f32[256,768]{1,0:T(8,128)} async-done(((f32[256,768]{1,0:T(8,128)}), f32[256,768]{1,0:T(8,128)}) %all-reduce.23.cloned.1.call-update) | async-done | bytes 786448 | tf_op jit(solution)/shard_map/psum | solution.py:14
  66.1 41.9 %all-reduce.37.cloned.1.call-done = (f32[256,768]{1,0:T(8,128)}, f32[128,768]{1,0:T(8,128)}) async-done(((f32[256,768]{1,0:T(8,128)}, f32[128,768]{1,0:T(8,128)}), (f32[256,768]{1,0:T(8,128)}, f32[128,768]{1,0:T(8,128)})) %all-reduce.37.cloned.1.call-update) | async-done | bytes 1179664 | tf_op jit(solution)/shard_map/psum | solution.py:14
  124.6 6.7 copy.152
  142.1 32.5 %all-gather.2.cloned.1.call-done = bf16[2,4096,384]{2,1,0:T(8,128)(2,1)} async-done(((bf16[2,256,384]{2,1,0:T(8,128)(2,1)}), bf16[2,4096,384]{2,1,0:T(8,128)(2,1)}) %all-gather.2.cloned.1.call-update) | async-done | bytes 6291472 | tf_op jit(solution)/shard_map/all_gather | solution.py:210
  185.6 9.1 eq.25
  196.5 14.8 fusion.4
  216.7 9.3 fusion.10
  236.1 22.5 %all-reduce.25.cloned.1.call-done = f32[128,768]{1,0:T(8,128)} async-done(((f32[128,768]{1,0:T(8,128)}), f32[128,768]{1,0:T(8,128)}) %all-reduce.25.cloned.1.call-update) | async-done | bytes 393232 | tf_op jit(solution)/shard_map/psum | solution.py:14
  270.2 23.3 %all-reduce.27.cloned.1.call-done = f32[128,768]{1,0:T(8,128)} async-done(((f32[128,768]{1,0:T(8,128)}), f32[128,768]{1,0:T(8,128)}) %all-reduce.27.cloned.1.call-update) | async-done | bytes 393232 | tf_op jit(solution)/shard_map/psum | solution.py:14
  305.0 24.5 %all-reduce.29.cloned.1.call-done = f32[128,768]{1,0:T(8,128)} async-done(((f32[128,768]{1,0:T(8,128)}), f32[128,768]{1,0:T(8,128)}) %all-reduce.29.cloned.1.call-update) | async-done | bytes 393232 | tf_op jit(solution)/shard_map/psum | solution.py:14
  335.5 11.7 fusion.12
  347.3 8.2 fusion.3
  360.5 10.7 pad_maximum_fusion
  371.3 134.9 %reduce-scatter.30.cloned.1.call-done = f32[2,256,384]{1,2,0:T(8,128)} async-done(((f32[2,4096,384]{1,2,0:T(8,128)}), f32[2,256,384]{1,2,0:T(8,128)}) %reduce-scatter.30.cloned.1.call-update) | async-done | bytes 786448 | tf_op jit(solution)/shard_map/reduce_scatter | solution.py:281
  516.3 26.8 %all-reduce.31.cloned.1.call-done = f32[256,768]{1,0:T(8,128)} async-done(((f32[256,768]{1,0:T(8,128)}), f32[256,768]{1,0:T(8,128)}) %all-reduce.31.cloned.1.call-update) | async-done | bytes 786448 | tf_op jit(solution)/shard_map/psum | solution.py:14
  553.7 42.8 %all-reduce.35.cloned.1.call-done = (f32[256,768]{1,0:T(8,128)}, f32[128,768]{1,0:T(8,128)}) async-done(((f32[256,768]{1,0:T(8,128)}, f32[128,768]{1,0:T(8,128)}), (f32[256,768]{1,0:T(8,128)}, f32[128,768]{1,0:T(8,128)})) %all-reduce.35.cloned.1.call-update) | async-done | bytes 1179664 | tf_op jit(solution)/shard_map/psum | solution.py:14
  689.1 62.0 %all-reduce.10 = (f32[768]{0:T(1024)}, f32[768]{0:T(1024)}, f32[768]{0:T(1024)}, f32[768]{0:T(1024)}, f32[768]{0:T(1024)}, /*index=5*/f32[768]{0:T(1024)}, f32[7...) all-reduce(f32[768]{0:T(1024)} %get-tuple-element.122, ...), channel_id=7, replica_groups=mesh['blk'=16,'tp'=2] {'blk'}, use_global_device_ids=true, to_apply=%region_46.47.clone | all-reduce | flops 7680 | bytes 61440
  767.7 23.8 %reduce-scatter.46.cloned.1.call-done = f32[384,48]{0,1:T(8,128)} async-done(((f32[384,768]{0,1:T(8,128)}), f32[384,48]{0,1:T(8,128)}) %reduce-scatter.46.cloned.1.call-update) | async-done | bytes 73744 | tf_op jit(solution)/shard_map/reduce_scatter | solution.py:349
  791.5 79.0 %reduce-scatter.48.cloned.1.call-done = f32[48,1536]{1,0:T(8,128)} async-done(((f32[768,1536]{1,0:T(8,128)}), f32[48,1536]{1,0:T(8,128)}) %reduce-scatter.48.cloned.1.call-update) | async-done | bytes 294928 | tf_op jit(solution)/shard_map/reduce_scatter | solution.py:352
  870.6 79.4 %reduce-scatter.50.cloned.1.call-done = f32[1536,48]{0,1:T(8,128)} async-done(((f32[1536,768]{0,1:T(8,128)}), f32[1536,48]{0,1:T(8,128)}) %reduce-scatter.50.cloned.1.call-update) | async-done | bytes 294928 | tf_op jit(solution)/shard_map/reduce_scatter | solution.py:353
  949.9 61.1 %reduce-scatter.42.cloned.1.call-done = f32[48,384]{1,0:T(8,128)} async-done(((f32[768,384]{1,0:T(8,128)}), f32[48,384]{1,0:T(8,128)}) %reduce-scatter.42.cloned.1.call-update) | async-done | bytes 73744 | tf_op jit(solution)/shard_map/reduce_scatter | solution.py:347
  1011.1 61.2 %reduce-scatter.44.cloned.1.call-done = f32[48,384]{1,0:T(8,128)} async-done(((f32[768,384]{1,0:T(8,128)}), f32[48,384]{1,0:T(8,128)}) %reduce-scatter.44.cloned.1.call-update) | async-done | bytes 73744 | tf_op jit(solution)/shard_map/reduce_scatter | solution.py:348
  1072.3 61.2 %reduce-scatter.52.cloned.1.call-done = f32[48,384]{1,0:T(8,128)} async-done(((f32[768,384]{1,0:T(8,128)}), f32[48,384]{1,0:T(8,128)}) %reduce-scatter.52.cloned.1.call-update) | async-done | bytes 73744
  1133.5 61.1 %reduce-scatter.54.cloned.1.call-done = f32[48,384]{1,0:T(8,128)} async-done(((f32[768,384]{1,0:T(8,128)}), f32[48,384]{1,0:T(8,128)}) %reduce-scatter.54.cloned.1.call-update) | async-done | bytes 73744
  1194.6 61.2 %reduce-scatter.56.cloned.1.call-done = f32[48,384]{1,0:T(8,128)} async-done(((f32[768,384]{1,0:T(8,128)}), f32[48,384]{1,0:T(8,128)}) %reduce-scatter.56.cloned.1.call-update) | async-done | bytes 73744
  1255.8 61.1 %reduce-scatter.32.cloned.1.call-done = f32[384,48]{0,1:T(8,128)} async-done(((f32[384,768]{0,1:T(8,128)}), f32[384,48]{0,1:T(8,128)}) %reduce-scatter.32.cloned.1.call-update) | async-done | bytes 73744 | tf_op jit(solution)/shard_map/reduce_scatter | solution.py:333
  1316.9 61.2 %reduce-scatter.58.cloned.1.call-done = f32[48,384]{1,0:T(8,128)} async-done(((f32[768,384]{1,0:T(8,128)}), f32[48,384]{1,0:T(8,128)}) %reduce-scatter.58.cloned.1.call-update) | async-done | bytes 73744
  1378.1 61.2 %reduce-scatter.60.cloned.1.call-done = f32[48,384]{1,0:T(8,128)} async-done(((f32[768,384]{1,0:T(8,128)}), f32[48,384]{1,0:T(8,128)}) %reduce-scatter.60.cloned.1.call-update) | async-done | bytes 73744
  1439.3 61.2 %reduce-scatter.62.cloned.1.call-done = f32[48,384]{1,0:T(8,128)} async-done(((f32[768,384]{1,0:T(8,128)}), f32[48,384]{1,0:T(8,128)}) %reduce-scatter.62.cloned.1.call-update) | async-done | bytes 73744
  1500.5 61.1 %reduce-scatter.38.cloned.1.call-done = f32[384,48]{0,1:T(8,128)} async-done(((f32[384,768]{0,1:T(8,128)}), f32[384,48]{0,1:T(8,128)}) %reduce-scatter.38.cloned.1.call-update) | async-done | bytes 73744 | tf_op jit(solution)/shard_map/reduce_scatter | solution.py:343
  1561.6 79.1 %reduce-scatter.34.cloned.1.call-done = f32[48,1536]{1,0:T(8,128)} async-done(((f32[768,1536]{1,0:T(8,128)}), f32[48,1536]{1,0:T(8,128)}) %reduce-scatter.34.cloned.1.call-update) | async-done | bytes 294928 | tf_op jit(solution)/shard_map/reduce_scatter | solution.py:336
  1640.7 79.4 %reduce-scatter.36.cloned.1.call-done = f32[1536,48]{0,1:T(8,128)} async-done(((f32[1536,768]{0,1:T(8,128)}), f32[1536,48]{0,1:T(8,128)}) %reduce-scatter.36.cloned.1.call-update) | async-done | bytes 294928 | tf_op jit(solution)/shard_map/reduce_scatter | solution.py:337
  (505 shorter events, 251.2 us)
Async XLA Ops:
  7.2 49.8 %copy-start = (bf16[768,1536]{1,0:T(8,128)(2,1)S(1)}, bf16[768,1536]{1,0:T(8,128)(2,1)}, u32[]{:S(2)}) copy-start(bf16[768,1536]{1,0:T(8,128)(2,1)} %param.44) | copy-start | bytes 7077892
  7.2 47.6 %all-reduce.23.cloned.1.call-start = ((), (), s32[]{:S(2)}) async-start(), calls=%async_computation.17 | async-start | bytes 1572864 | tf_op jit(solution)/shard_map/psum | solution.py:14
  17.7 90.3 %all-reduce.37.cloned.1.call-start = ((), (), s32[]{:S(2)}) async-start(), calls=%async_computation.42 | async-start | bytes 2359296 | tf_op jit(solution)/shard_map/psum | solution.py:14
  56.1 51.9 %copy-start.85 = (f32[256]{0:T(256)}, f32[256]{0:T(256)S(1)}, u32[]{:S(2)}) copy-start(f32[256]{0:T(256)S(1)} %broadcast_multiply_fusion.1) | copy-start | bytes 3076
  64.8 109.9 %all-gather.2.cloned.1.call-start = ((), (), s32[]{:S(2)}) async-start(), calls=%async_computation.18 | async-start | bytes 6684672 | tf_op jit(solution)/shard_map/all_gather | solution.py:210
  66.1 43.7 %copy-start.82 = (f32[768]{0:T(1024)}, f32[768]{0:T(1024)S(1)}, u32[]{:S(2)}) copy-start(f32[768]{0:T(1024)S(1)} %convert_element_type.247) | copy-start | bytes 9220
  112.5 146.1 %all-reduce.25.cloned.1.call-start = ((), (), s32[]{:S(2)}) async-start(), calls=%async_computation.19 | async-start | bytes 786432 | tf_op jit(solution)/shard_map/psum | solution.py:14
  234.1 59.4 %all-reduce.27.cloned.1.call-start = ((), (), s32[]{:S(2)}) async-start(), calls=%async_computation.20 | async-start | bytes 786432 | tf_op jit(solution)/shard_map/psum | solution.py:14
  267.6 62.0 %all-reduce.29.cloned.1.call-start = ((), (), s32[]{:S(2)}) async-start(), calls=%async_computation.21 | async-start | bytes 786432 | tf_op jit(solution)/shard_map/psum | solution.py:14
  303.7 202.5 %reduce-scatter.30.cloned.1.call-start = ((), (), s32[]{:S(2)}) async-start(), calls=%async_computation.22 | async-start | bytes 13369344 | tf_op jit(solution)/shard_map/reduce_scatter | solution.py:281
  335.5 11.8 copy-start.15
  335.5 11.8 copy-start.91
  371.3 171.9 %all-reduce.31.cloned.1.call-start = ((), (), s32[]{:S(2)}) async-start(), calls=%async_computation.23 | async-start | bytes 1572864 | tf_op jit(solution)/shard_map/psum | solution.py:14
  509.5 87.0 %all-reduce.35.cloned.1.call-start = ((), (), s32[]{:S(2)}) async-start(), calls=%async_computation.41 | async-start | bytes 2359296 | tf_op jit(solution)/shard_map/psum | solution.py:14
  553.3 210.4 %all-reduce.33.cloned.1.call-start = ((), (), s32[]{:S(2)}) async-start(), calls=%async_computation.40 | async-start | bytes 2359296 | tf_op jit(solution)/shard_map/psum | solution.py:14
  624.8 142.9 %reduce-scatter.40.cloned.1.call-start = ((), (), s32[]{:S(2)}) async-start(), calls=%async_computation.28 | async-start | bytes 1253376 | tf_op jit(solution)/shard_map/reduce_scatter | solution.py:346
  627.4 164.1 %reduce-scatter.46.cloned.1.call-start = ((), (), s32[]{:S(2)}) async-start(), calls=%async_computation.31 | async-start | bytes 1253376 | tf_op jit(solution)/shard_map/reduce_scatter | solution.py:349
  629.9 240.6 %reduce-scatter.48.cloned.1.call-start = ((), (), s32[]{:S(2)}) async-start(), calls=%async_computation.32 | async-start | bytes 5013504 | tf_op jit(solution)/shard_map/reduce_scatter | solution.py:352
  634.3 315.6 %reduce-scatter.50.cloned.1.call-start = ((), (), s32[]{:S(2)}) async-start(), calls=%async_computation.33 | async-start | bytes 5013504 | tf_op jit(solution)/shard_map/reduce_scatter | solution.py:353
  639.2 371.9 %reduce-scatter.42.cloned.1.call-start = ((), (), s32[]{:S(2)}) async-start(), calls=%async_computation.29 | async-start | bytes 1253376 | tf_op jit(solution)/shard_map/reduce_scatter | solution.py:347
  641.7 430.6 %reduce-scatter.44.cloned.1.call-start = ((), (), s32[]{:S(2)}) async-start(), calls=%async_computation.30 | async-start | bytes 1253376 | tf_op jit(solution)/shard_map/reduce_scatter | solution.py:348
  644.3 489.2 %reduce-scatter.52.cloned.1.call-start = ((), (), s32[]{:S(2)}) async-start(), calls=%async_computation.34 | async-start | bytes 1253376
  649.4 545.2 %reduce-scatter.54.cloned.1.call-start = ((), (), s32[]{:S(2)}) async-start(), calls=%async_computation.35 | async-start | bytes 1253376
  654.5 601.3 %reduce-scatter.56.cloned.1.call-start = ((), (), s32[]{:S(2)}) async-start(), calls=%async_computation.36 | async-start | bytes 1253376
  659.5 657.4 %reduce-scatter.32.cloned.1.call-start = ((), (), s32[]{:S(2)}) async-start(), calls=%async_computation.24 | async-start | bytes 1253376 | tf_op jit(solution)/shard_map/reduce_scatter | solution.py:333
  662.4 715.7 %reduce-scatter.58.cloned.1.call-start = ((), (), s32[]{:S(2)}) async-start(), calls=%async_computation.37 | async-start | bytes 1253376
  666.5 772.8 %reduce-scatter.60.cloned.1.call-start = ((), (), s32[]{:S(2)}) async-start(), calls=%async_computation.38 | async-start | bytes 1253376
  670.6 829.9 %reduce-scatter.62.cloned.1.call-start = ((), (), s32[]{:S(2)}) async-start(), calls=%async_computation.39 | async-start | bytes 1253376
  674.9 886.7 %reduce-scatter.38.cloned.1.call-start = ((), (), s32[]{:S(2)}) async-start(), calls=%async_computation.27 | async-start | bytes 1253376 | tf_op jit(solution)/shard_map/reduce_scatter | solution.py:343
  677.4 963.3 %reduce-scatter.34.cloned.1.call-start = ((), (), s32[]{:S(2)}) async-start(), calls=%async_computation.25 | async-start | bytes 5013504 | tf_op jit(solution)/shard_map/reduce_scatter | solution.py:336
  681.8 1038.3 %reduce-scatter.36.cloned.1.call-start = ((), (), s32[]{:S(2)}) async-start(), calls=%async_computation.26 | async-start | bytes 5013504 | tf_op jit(solution)/shard_map/reduce_scatter | solution.py:337
  687.1 78.4 %copy-start.14 = (f32[256,768]{1,0:T(8,128)S(1)}, f32[256,768]{1,0:T(8,128)}, u32[]{:S(2)}) copy-start(f32[256,768]{1,0:T(8,128)} %copy-done.13) | copy-start | bytes 2359300
  (137 other events, 365.7 us)
Sparse Core Ops, SparseCore 0:
  17.8 36.9 all-reduce.22
  64.9 43.0 all-reduce.36
  112.6 61.9 all-gather.1
  234.3 24.2 all-reduce.24
  267.7 25.7 all-reduce.26
  303.8 25.7 all-reduce.28
  371.4 134.7 reduce-scatter.29
  509.7 33.4 all-reduce.30
  553.4 43.0 all-reduce.34
  624.9 43.0 all-reduce.32
  672.2 58.1 reduce-scatter.39
  734.5 56.9 reduce-scatter.45
  795.9 74.5 reduce-scatter.47
  875.3 74.5 reduce-scatter.49
  954.0 57.0 reduce-scatter.41
  1015.1 57.1 reduce-scatter.43
  1076.3 57.0 reduce-scatter.51
  1137.5 56.9 reduce-scatter.53
  1198.7 56.9 reduce-scatter.55
  1259.8 56.9 reduce-scatter.31
  1321.1 56.9 reduce-scatter.57
  1382.3 56.9 reduce-scatter.59
  1443.5 56.9 reduce-scatter.61
  1504.6 57.0 reduce-scatter.37
  1566.1 74.5 reduce-scatter.33
  1645.5 74.5 reduce-scatter.35
where the time goes:
time: 1740 us; the launch traced here: 1730 us
  waiting for transfers between devices  1330 us (76%)
  matrix products  161 us (9%)
  local copies, waits for them, and re-layouts  97.8 us (6%)
  blocking collectives  62 us (4%)
  other arithmetic  60.2 us (3%)
    unnamed x32, waiting for transfers between devices  368 us
    psum x8, waiting for transfers between devices, head_sum(): return lax.psum(partial_value, 'tp')  206 us
    reduce_scatter x1, waiting for transfers between devices, on_device(): lax.psum_scatter(grad_store, 'blk', scatter_dimension=1, tiled=True)  135 us
    reduce_scatter x1, waiting for transfers between devices, on_device(): lax.psum_scatter(grad_dec_down, 'blk', scatter_dimension=1, tiled=True)  79.4 us
    reduce_scatter x1, waiting for transfers between devices, on_device(): lax.psum_scatter(grad_enc_down, 'blk', scatter_dimension=1, tiled=True)  79.4 us
    reduce_scatter x1, waiting for transfers between devices, on_device(): lax.psum_scatter(grad_enc_up, 'blk', scatter_dimension=0, tiled=True)  79.1 us
    reduce_scatter x1, waiting for transfers between devices, on_device(): lax.psum_scatter(grad_dec_up, 'blk', scatter_dimension=0, tiled=True)  79 us
    unnamed x1, blocking collectives  62 us
  transfers between devices with their start and end apart: 26, of which 24 were waited for; matrix products, arithmetic and copies ran while one was open for 8% of the time, Pallas kernels for 0%

commit v1 on v0

v1 whole, which is shorter than its diff:
```python
import functools

import jax
import jax.numpy as jnp
from jax import lax
from jax.experimental import pallas as pl
from jax.experimental.pallas import tpu as pltpu
from jax.sharding import PartitionSpec as P

HD = 64
PAIR = 2 * HD
NEG_FILL = -1e30
EPS_NORM = 1e-05
SCALE = 0.125
BF = jnp.bfloat16
F32 = jnp.float32
VMEM_LIMIT = 48 * 2**20
ROWS = 64


def nn(a, b):
    return lax.dot_general(a, b, (((1,), (0,)), ((), ())), preferred_element_type=F32)


def nt(a, b):
    return lax.dot_general(a, b, (((1,), (1,)), ((), ())), preferred_element_type=F32)


def tn(a, b):
    return lax.dot_general(a, b, (((0,), (0,)), ((), ())), preferred_element_type=F32)


def whole(body, name, outs, *args, smem=0, flops=0):
    moved = sum(a.size * a.dtype.itemsize for a in args)
    moved += sum(jnp.dtype(d).itemsize * functools.reduce(lambda x, y: x * y, s, 1) for s, d in outs)
    return pl.pallas_call(
        body,
        name=name,
        out_shape=[jax.ShapeDtypeStruct(s, d) for s, d in outs],
        in_specs=[pl.BlockSpec(memory_space=pltpu.SMEM)] * smem
        + [pl.BlockSpec(memory_space=pltpu.VMEM)] * (len(args) - smem),
        out_specs=[pl.BlockSpec(memory_space=pltpu.VMEM)] * len(outs),
        compiler_params=pltpu.CompilerParams(vmem_limit_bytes=VMEM_LIMIT),
        cost_estimate=pl.CostEstimate(flops=flops, bytes_accessed=moved, transcendentals=0),
    )(*args)


def norm_parts(v):
    center = v - jnp.mean(v, -1, keepdims=True)
    r = lax.rsqrt(jnp.mean(center * center, -1, keepdims=True) + EPS_NORM)
    return center * r, r


def norm_back(v, gain, dy):
    xhat, r = norm_parts(v)
    gdy = gain * dy
    dv = r * (gdy - jnp.mean(gdy, -1, keepdims=True) - xhat * jnp.mean(gdy * xhat, -1, keepdims=True))
    return dv, jnp.sum(dy * xhat, 0, keepdims=True), jnp.sum(dy, 0, keepdims=True)


def row_of(par_ref, i):
    return par_ref[i : i + 1, :].astype(F32)


def low_half(shape, dim):
    return lax.broadcasted_iota(jnp.int32, shape, dim) < HD


def stacked(t2):
    first = low_half(t2.shape, 1)
    zero = jnp.zeros_like(t2)
    return jnp.concatenate([jnp.where(first, t2, zero), jnp.where(first, zero, t2)], 0)


def unstacked(tT):
    R = tT.shape[1] // 2
    first = low_half((PAIR, R), 0)
    return jnp.where(first, tT[:, :R], tT[:, R:]).T


def causal_mask(R, length):
    key = lax.broadcasted_iota(jnp.int32, (R, 2 * R), 0)
    lane = lax.broadcasted_iota(jnp.int32, (R, 2 * R), 1)
    query = jnp.where(lane >= R, lane - R, lane)
    return (key <= query) & (key < length)


def local_weights(k2, qq, allowed):
    sT = nt(k2, qq)
    if allowed is not None:
        sT = jnp.where(allowed, sT, NEG_FILL)
    p = jnp.exp(sT - jnp.max(sT, 0, keepdims=True))
    return p * (1.0 / jnp.sum(p, 0, keepdims=True))


def gelu_parts(h):
    cdf = 0.5 * (1.0 + lax.erf(h * 0.7071067811865476))
    pdf = 0.3989422804014327 * jnp.exp(-0.5 * h * h)
    return h * cdf, cdf + h * pdf


def attend_fwd_body(causal, *refs):
    if causal:
        len_ref, refs = refs[0], refs[1:]
    x_ref, wq, wk, wv, wm, q_ref, k_ref, v_ref, o_ref, part_ref = refs
    x = x_ref[...]
    R = x.shape[0]
    q_ref[...] = (nn(x, wq[...]) * SCALE).astype(BF)
    k_ref[...] = nn(x, wk[...]).astype(BF)
    v_ref[...] = nn(x, wv[...]).astype(BF)
    allowed = causal_mask(R, len_ref[0]) if causal else None
    for c in range(0, q_ref.shape[1], PAIR):
        sl = slice(c, c + PAIR)
        w = local_weights(k_ref[:, sl], stacked(q_ref[:, sl]), allowed).astype(BF)
        o_ref[:, sl] = unstacked(tn(v_ref[:, sl], w)).astype(BF)
    part_ref[...] = nn(o_ref[...], wm[...]).astype(BF)


def attend_fwd(x, wq, wk, wv, wm, length=None):
    R, D = x.shape
    C = wq.shape[1]
    args = (x, wq, wk, wv, wm)
    causal = length is not None
    if causal:
        args = (length,) + args
    return whole(
        functools.partial(attend_fwd_body, causal),
        "attend_fwd",
        [((R, C), BF)] * 4 + [((R, D), BF)],
        *args,
        smem=int(causal),
        flops=8 * R * D * C + 8 * R * R * C,
    )


def ffn_fwd_body(g, x_ref, own, oth, par, wu, wd, v_ref, u_ref, low_ref, act_ref, gp_ref, part_ref):
    R = x_ref.shape[0]
    gain, shift = row_of(par, g), row_of(par, g + 1)
    for r in range(0, R, ROWS):
        s = slice(r, r + ROWS)
        v = x_ref[s, :].astype(F32) + (own[s, :].astype(F32) + oth[s, :].astype(F32))
        xhat, _ = norm_parts(v)
        u = xhat * gain + shift
        v_ref[s, :] = v
        u_ref[s, :] = u
        low_ref[s, :] = u.astype(BF)
    low = low_ref[...]
    for c in range(0, wu.shape[1], 256):
        sl = slice(c, c + 256)
        a, gp = gelu_parts(nn(low, wu[:, sl]))
        act_ref[:, sl] = a.astype(BF)
        gp_ref[:, sl] = gp.astype(BF)
    part_ref[...] = nn(act_ref[...], wd[...]).astype(BF)


def ffn_fwd(g, x, own, oth, par, wu, wd):
    R, D = x.shape
    FF = wu.shape[1]
    return whole(
        functools.partial(ffn_fwd_body, g),
        "ffn_fwd",
        [((R, D), F32), ((R, D), F32), ((R, D), BF), ((R, FF), BF), ((R, FF), BF), ((R, D), BF)],
        x, own, oth, par, wu, wd,
        flops=4 * R * D * FF,
    )


def order_matrix(R):
    t = lax.broadcasted_iota(jnp.int32, (R, R), 0)
    col = lax.broadcasted_iota(jnp.int32, (R, R), 1)
    src = jnp.where(t < R // 2, 2 * t, 2 * t - (R - 1))
    return (src == col).astype(F32).astype(BF)


def store_body(g, u_ref, own, oth, par, wk, wv, v_ref, enc_ref, low_ref, kv_ref):
    R = u_ref.shape[0]
    gain, shift = row_of(par, g), row_of(par, g + 1)
    for r in range(0, R, ROWS):
        s = slice(r, r + ROWS)
        v = u_ref[s, :] + (own[s, :].astype(F32) + oth[s, :].astype(F32))
        xhat, _ = norm_parts(v)
        v_ref[s, :] = v
        enc_ref[s, :] = xhat * gain + shift
    low_ref[...] = nn(order_matrix(R), enc_ref[...].astype(BF)).astype(BF)
    low = low_ref[...]
    kv_ref[0] = nn(low, wk[...]).astype(BF)
    kv_ref[1] = nn(low, wv[...]).astype(BF)


def store_fwd(g, u, own, oth, par, wk, wv):
    R, D = u.shape
    C = wk.shape[1]
    return whole(
        functools.partial(store_body, g),
        "store_fwd",
        [((R, D), F32), ((R, D), F32), ((R, D), BF), ((2, R, C), BF)],
        u, own, oth, par, wk, wv,
        flops=4 * R * D * C + 2 * R * R * D,
    )


def cross_q_body(g, x_ref, own, oth, par, wq, v_ref, u_ref, low_ref, q_ref):
    R = x_ref.shape[0]
    gain, shift = row_of(par, g), row_of(par, g + 1)
    for r in range(0, R, ROWS):
        s = slice(r, r + ROWS)
        v = x_ref[s, :].astype(F32) + (own[s, :].astype(F32) + oth[s, :].astype(F32))
        xhat, _ = norm_parts(v)
        u = xhat * gain + shift
        v_ref[s, :] = v
        u_ref[s, :] = u
        low_ref[s, :] = u.astype(BF)
    q_ref[...] = (nn(low_ref[...], wq[...]) * SCALE).astype(BF)


def cross_q(g, x, own, oth, par, wq):
    R, D = x.shape
    C = wq.shape[1]
    return whole(
        functools.partial(cross_q_body, g),
        "cross_q",
        [((R, D), F32), ((R, D), F32), ((R, D), BF), ((R, C), BF)],
        x, own, oth, par, wq,
        flops=2 * R * D * C,
    )


def picks_body(pick_ref, band_ref, out_ref):
    g = pl.program_id(0)
    heads, picked, R = pick_ref.shape
    half = out_ref.shape[2]
    for h in range(heads):
        rel = g - band_ref[h : h + 1, :]
        got = jnp.full((half, R), -1.0, F32)
        for b in range(picked // half):
            got = jnp.where(rel == b, pick_ref[h, b * half : (b + 1) * half, :], got)
        out_ref[0, h // 2, :, (h % 2) * R : (h % 2 + 1) * R] = got


def picks(retrieved, band_start, groups, half):
    R, heads, picked = retrieved.shape
    pick = (retrieved & 1).astype(F32).transpose(1, 2, 0)
    band = band_start.T
    return pl.pallas_call(
        picks_body,
        name="picks",
        grid=(groups,),
        out_shape=jax.ShapeDtypeStruct((groups, heads // 2, half, 2 * R), F32),
        in_specs=[
            pl.BlockSpec((heads, picked, R), lambda g: (0, 0, 0)),
            pl.BlockSpec((heads, R), lambda g: (0, 0)),
        ],
        out_specs=pl.BlockSpec((1, heads // 2, half, 2 * R), lambda g: (g, 0, 0, 0)),
        compiler_params=pltpu.CompilerParams(vmem_limit_bytes=VMEM_LIMIT),
    )(pick, band)


def chosen_scores(k2, qq, a):
    half = a.shape[0]
    sT = nt(k2, qq)
    s = jnp.where(a > 0.5, sT[half:], sT[:half])
    return jnp.where(a < -0.5, NEG_FILL, s)


def spread(p, a):
    zero = jnp.zeros_like(p)
    even = jnp.where(a == 0.0, p, zero).astype(BF)
    odd = jnp.where(a == 1.0, p, zero).astype(BF)
    return jnp.concatenate([even, odd], 0)


def cross_fwd_body(first, gid_ref, q_ref, *refs):
    kv, a_refs, refs = refs[:4], refs[4:8], refs[8:]
    if first:
        m_ref, l_ref, acc_ref = refs
    else:
        m_in, l_in, acc_in, m_ref, l_ref, acc_ref = refs

    @pl.when(pl.program_id(0) == 0)
    def _():
        if first:
            m_ref[...] = jnp.full(m_ref.shape, NEG_FILL, F32)
            l_ref[...] = jnp.zeros(l_ref.shape, F32)
            acc_ref[...] = jnp.zeros(acc_ref.shape, F32)
        else:
            m_ref[...] = m_in[...]
            l_ref[...] = l_in[...]
            acc_ref[...] = acc_in[...]

    for hp in range(acc_ref.shape[0]):
        sl = slice(hp * PAIR, (hp + 1) * PAIR)
        qq = stacked(q_ref[:, sl])
        scores = [chosen_scores(kv[j][0, 0, :, sl], qq, a_refs[j][0, hp]) for j in range(4)]
        old = m_ref[hp : hp + 1, :]
        top = functools.reduce(jnp.maximum, [jnp.max(s, 0, keepdims=True) for s in scores], old)
        fade = jnp.exp(old - top)
        total = l_ref[hp : hp + 1, :] * fade
        acc = acc_ref[hp] * fade
        for j in range(4):
            a = a_refs[j][0, hp]
            p = jnp.where(a < -0.5, 0.0, jnp.exp(scores[j] - top))
            total = total + jnp.sum(p, 0, keepdims=True)
            acc = acc + tn(kv[j][0, 1, :, sl], spread(p, a))
        m_ref[hp : hp + 1, :] = top
        l_ref[hp : hp + 1, :] = total
        acc_ref[hp] = acc


def kv_specs(kv, a):
    rows, C = kv[0].shape[2:]
    specs = [pl.BlockSpec((1, 2, rows, C), lambda i, gid: (i, 0, 0, 0)) for _ in range(4)]
    for j in range(4):
        specs.append(
            pl.BlockSpec((1,) + a.shape[1:], functools.partial(lambda j, i, gid: (gid[4 * i + j], 0, 0, 0), j))
        )
    return specs


def fixed(shape):
    return pl.BlockSpec(shape, lambda i, gid: (0,) * len(shape))


def cross_fwd(gid, q, kv, a, state):
    R, C = q.shape
    pairs = C // PAIR
    hi = kv[0].shape[0]
    rows = kv[0].shape[2]
    shapes = [(8, 2 * R), (8, 2 * R), (pairs, PAIR, 2 * R)]
    first = state is None
    state = () if first else tuple(state)
    return pl.pallas_call(
        functools.partial(cross_fwd_body, first),
        name="cross_fwd",
        grid_spec=pltpu.PrefetchScalarGridSpec(
            num_scalar_prefetch=1,
            grid=(hi,),
            in_specs=[fixed(q.shape)] + kv_specs(kv, a) + [fixed(s.shape) for s in state],
            out_specs=[fixed(s) for s in shapes],
        ),
        out_shape=[jax.ShapeDtypeStruct(s, F32) for s in shapes],
        compiler_params=pltpu.CompilerParams(vmem_limit_bytes=VMEM_LIMIT),
        cost_estimate=pl.CostEstimate(
            flops=hi * 4 * 8 * R * rows * C, bytes_accessed=hi * 4 * 4 * rows * C, transcendentals=0
        ),
    )(gid, q, *kv, *([a] * 4), *state)


def cross_mix_body(m_ref, l_ref, acc_ref, wm, log_ref, of_ref, o_ref, part_ref):
    pairs = acc_ref.shape[0]
    log_ref[...] = jnp.zeros(log_ref.shape, F32)
    for hp in range(pairs):
        sl = slice(hp * PAIR, (hp + 1) * PAIR)
        total = l_ref[hp : hp + 1, :]
        log_ref[hp : hp + 1, :] = m_ref[hp : hp + 1, :] + jnp.log(total)
        o = unstacked(acc_ref[hp] * (1.0 / total))
        of_ref[:, sl] = o
        o_ref[:, sl] = o.astype(BF)
    part_ref[...] = nn(o_ref[...], wm[...]).astype(BF)


def cross_mix_fwd(m, l, acc, wm):
    R2 = m.shape[1]
    C, D = wm.shape
    R = R2 // 2
    return whole(
        cross_mix_body,
        "cross_mix",
        [((8, R2), F32), ((R, C), F32), ((R, C), BF), ((R, D), BF)],
        m, l, acc, wm,
        flops=2 * R * C * D,
    )


def ffn_back_rest(dlow_ref, gp_ref, wu, wd, dh_ref, part_ref):
    low = dlow_ref[...]
    for c in range(0, wu.shape[1], 256):
        sl = slice(c, c + 256)
        dh_ref[:, sl] = (nt(low, wd[sl, :]) * gp_ref[:, sl].astype(F32)).astype(BF)
    part_ref[...] = nt(dh_ref[...], wu[...]).astype(BF)


def last_body(g, u_ref, own, oth, cot, par, gp_ref, wu, wd, out_ref, dv_ref, dlow_ref, dh_ref, gg_ref, part_ref):
    R = u_ref.shape[0]
    gain, shift = row_of(par, g), row_of(par, g + 1)
    gg_ref[...] = jnp.zeros(gg_ref.shape, F32)
    for r in range(0, R, ROWS):
        s = slice(r, r + ROWS)
        v = u_ref[s, :] + (own[s, :].astype(F32) + oth[s, :].astype(F32))
        xhat, _ = norm_parts(v)
        out_ref[s, :] = xhat * gain + shift
        dv, dg, db = norm_back(v, gain, cot[s, :].astype(F32))
        dv_ref[s, :] = dv
        dlow_ref[s, :] = dv.astype(BF)
        gg_ref[0:1, :] += dg
        gg_ref[1:2, :] += db
    ffn_back_rest(dlow_ref, gp_ref, wu, wd, dh_ref, part_ref)


def last_fwd_back(g, u, own, oth, cot, par, gp, wu, wd):
    R, D = u.shape
    FF = wu.shape[1]
    return whole(
        functools.partial(last_body, g),
        "last_fwd_back",
        [((R, D), F32), ((R, D), F32), ((R, D), BF), ((R, FF), BF), ((8, D), F32), ((R, D), BF)],
        u, own, oth, cot, par, gp, wu, wd,
        flops=4 * R * D * FF,
    )


def ffn_back_body(g, own, oth, v_ref, par, gp_ref, wu, wd, dv_ref, dlow_ref, dh_ref, gg_ref, part_ref):
    R = v_ref.shape[0]
    gain = row_of(par, g)
    gg_ref[...] = jnp.zeros(gg_ref.shape, F32)
    for r in range(0, R, ROWS):
        s = slice(r, r + ROWS)
        dy = own[s, :].astype(F32) + oth[s, :].astype(F32)
        dv, dg, db = norm_back(v_ref[s, :], gain, dy)
        dv_ref[s, :] = dv
        dlow_ref[s, :] = dv.astype(BF)
        gg_ref[0:1, :] += dg
        gg_ref[1:2, :] += db
    ffn_back_rest(dlow_ref, gp_ref, wu, wd, dh_ref, part_ref)


def ffn_back(g, own, oth, v, par, gp, wu, wd):
    R, D = v.shape
    FF = wu.shape[1]
    return whole(
        functools.partial(ffn_back_body, g),
        "ffn_back",
        [((R, D), F32), ((R, D), BF), ((R, FF), BF), ((8, D), F32), ((R, D), BF)],
        own, oth, v, par, gp, wu, wd,
        flops=4 * R * D * FF,
    )


def branch_back(g, dres, own, oth, v_ref, par, dv_ref, dlow_ref, gg_ref):
    R = v_ref.shape[0]
    gain = row_of(par, g)
    gg_ref[...] = jnp.zeros(gg_ref.shape, F32)
    for r in range(0, R, ROWS):
        s = slice(r, r + ROWS)
        dy = dres[s, :] + (own[s, :].astype(F32) + oth[s, :].astype(F32))
        dv, dg, db = norm_back(v_ref[s, :], gain, dy)
        dv_ref[s, :] = dv
        dlow_ref[s, :] = dv.astype(BF)
        gg_ref[0:1, :] += dg
        gg_ref[1:2, :] += db


def cross_mix_back_body(g, dres, own, oth, v_ref, par, of_ref, wm, dv_ref, dlow_ref, do_ref, delta_ref, gg_ref):
    branch_back(g, dres, own, oth, v_ref, par, dv_ref, dlow_ref, gg_ref)
    do_ref[...] = nt(dlow_ref[...], wm[...]).astype(BF)
    delta_ref[...] = jnp.zeros(delta_ref.shape, F32)
    for hp in range(do_ref.shape[1] // PAIR):
        sl = slice(hp * PAIR, (hp + 1) * PAIR)
        prod = (do_ref[:, sl].astype(F32) * of_ref[:, sl]).T
        delta_ref[hp : hp + 1, :] = jnp.concatenate(
            [jnp.sum(prod[:HD], 0, keepdims=True), jnp.sum(prod[HD:], 0, keepdims=True)], 1
        )


def cross_mix_back(g, dres, own, oth, v, par, of, wm):
    R, D = v.shape
    C = wm.shape[0]
    return whole(
        functools.partial(cross_mix_back_body, g),
        "cross_mix_back",
        [((R, D), F32), ((R, D), BF), ((R, C), BF), ((8, 2 * R), F32), ((8, D), F32)],
        dres, own, oth, v, par, of, wm,
        flops=2 * R * D * C,
    )


def cross_back_body(first, gid_ref, q_ref, do_ref, log_ref, delta_ref, *refs):
    kv, a_refs, refs = refs[:4], refs[4:8], refs[8:]
    if first:
        dq_ref, keep_ref, send_ref = refs
    else:
        dq_in, dq_ref, keep_ref, send_ref = refs

    @pl.when(pl.program_id(0) == 0)
    def _():
        if first:
            dq_ref[...] = jnp.zeros(dq_ref.shape, F32)
        else:
            dq_ref[...] = dq_in[...]

    outs = ((keep_ref, 0), (keep_ref, 1), (send_ref, 0), (send_ref, 1))
    for hp in range(dq_ref.shape[0]):
        sl = slice(hp * PAIR, (hp + 1) * PAIR)
        qq = stacked(q_ref[:, sl])
        dd = stacked(do_ref[:, sl])
        log_total = log_ref[hp : hp + 1, :]
        delta = delta_ref[hp : hp + 1, :]
        dq = dq_ref[hp]
        for j in range(4):
            a = a_refs[j][0, hp]
            half = a.shape[0]
            k2 = kv[j][0, 0, :, sl]
            p = jnp.exp(chosen_scores(k2, qq, a) - log_total)
            daT = nt(kv[j][0, 1, :, sl], dd)
            ds = p * (jnp.where(a > 0.5, daT[half:], daT[:half]) - delta)
            dsT = spread(ds, a)
            out_ref, y = outs[j]
            out_ref[0, y, 0, :, sl] = nn(dsT, qq).astype(BF)
            out_ref[0, y, 1, :, sl] = nn(spread(p, a), dd).astype(BF)
            dq = dq + tn(k2, dsT)
        dq_ref[hp] = dq


def cross_back(gid, q, do, log_total, delta, kv, a, dq):
    R, C = q.shape
    pairs = C // PAIR
    hi, _, rows, _ = kv[0].shape
    first = dq is None
    extra = () if first else (dq,)
    dq_shape = (pairs, PAIR, 2 * R)
    grad_spec = pl.BlockSpec((1, 2, 2, rows, C), lambda i, gid: (i, 0, 0, 0, 0))
    grad_shape = jax.ShapeDtypeStruct((hi, 2, 2, rows, C), BF)
    return pl.pallas_call(
        functools.partial(cross_back_body, first),
        name="cross_back",
        grid_spec=pltpu.PrefetchScalarGridSpec(
            num_scalar_prefetch=1,
            grid=(hi,),
            in_specs=[fixed(q.shape), fixed(do.shape), fixed(log_total.shape), fixed(delta.shape)]
            + kv_specs(kv, a)
            + [fixed(e.shape) for e in extra],
            out_specs=[fixed(dq_shape), grad_spec, grad_spec],
        ),
        out_shape=[jax.ShapeDtypeStruct(dq_shape, F32), grad_shape, grad_shape],
        compiler_params=pltpu.CompilerParams(vmem_limit_bytes=VMEM_LIMIT),
        cost_estimate=pl.CostEstimate(
            flops=hi * 4 * 20 * R * rows * C, bytes_accessed=hi * 4 * 8 * rows * C, transcendentals=0
        ),
    )(gid, q, do, log_total, delta, *kv, *([a] * 4), *extra)


def cross_q_back_body(dq_in, wq, dq_ref, part_ref):
    for hp in range(dq_in.shape[0]):
        sl = slice(hp * PAIR, (hp + 1) * PAIR)
        dq_ref[:, sl] = (unstacked(dq_in[hp]) * SCALE).astype(BF)
    part_ref[...] = nt(dq_ref[...], wq[...]).astype(BF)


def cross_q_back(dq, wq):
    D, C = wq.shape
    R = dq.shape[2] // 2
    return whole(
        cross_q_back_body, "cross_q_back", [((R, C), BF), ((R, D), BF)], dq, wq, flops=2 * R * D * C
    )


def store_back_body(*refs):
    n = len(refs) - 4
    wk, wv, dkv_ref, part_ref = refs[n:]
    _, _, R, C = refs[0].shape
    for i in range(2):
        total = functools.reduce(lambda x, y: x + y, [t[0, i].astype(F32) for t in refs[:n]])
        dkv_ref[:, i * C : (i + 1) * C] = total.astype(BF)
    part = nt(dkv_ref[:, :C], wk[...]) + nt(dkv_ref[:, C:], wv[...])
    part_ref[...] = tn(order_matrix(R), part.astype(BF)).astype(BF)


def store_back(terms, wk, wv):
    D, C = wk.shape
    R = terms[0].shape[2]
    return whole(
        store_back_body, "store_back", [((R, 2 * C), BF), ((R, D), BF)], *terms, wk, wv, flops=4 * R * D * C
    )


def attend_back_body(causal, g, *refs):
    if causal:
        len_ref, refs = refs[0], refs[1:]
    (dres, own, oth, v1_ref, par, q_ref, k_ref, v_ref, wq, wk, wv, wm) = refs[:12]
    (dv_ref, dlow_ref, dqkv_ref, gg_ref, part_ref) = refs[12:]
    branch_back(g, dres, own, oth, v1_ref, par, dv_ref, dlow_ref, gg_ref)
    R = v1_ref.shape[0]
    C = wq.shape[1]
    do = nt(dlow_ref[...], wm[...]).astype(BF)
    allowed = causal_mask(R, len_ref[0]) if causal else None
    for c in range(0, C, PAIR):
        sl = slice(c, c + PAIR)
        k2 = k_ref[:, sl]
        qq = stacked(q_ref[:, sl])
        dd = stacked(do[:, sl])
        w = local_weights(k2, qq, allowed)
        daT = nt(v_ref[:, sl], dd)
        ds = (w * (daT - jnp.sum(w * daT, 0, keepdims=True))).astype(BF)
        dqkv_ref[:, c : c + PAIR] = (unstacked(tn(k2, ds)) * SCALE).astype(BF)
        dqkv_ref[:, C + c : C + c + PAIR] = nn(ds, qq).astype(BF)
        dqkv_ref[:, 2 * C + c : 2 * C + c + PAIR] = nn(w.astype(BF), dd).astype(BF)
    part = nt(dqkv_ref[:, :C], wq[...]) + nt(dqkv_ref[:, C : 2 * C], wk[...]) + nt(dqkv_ref[:, 2 * C :], wv[...])
    part_ref[...] = part.astype(BF)


def attend_back(g, dres, own, oth, v1, par, kept, weights, length=None):
    R, D = v1.shape
    q, k, v = kept
    C = q.shape[1]
    args = (dres, own, oth, v1, par, q, k, v) + tuple(weights)
    causal = length is not None
    if causal:
        args = (length,) + args
    return whole(
        functools.partial(attend_back_body, causal, g),
        "attend_back",
        [((R, D), F32), ((R, D), BF), ((R, 3 * C), BF), ((8, D), F32), ((R, D), BF)],
        *args,
        smem=int(causal),
        flops=8 * R * D * C + 20 * R * R * C,
    )


def weight_body(plan, n_in, idx_ref, *refs):
    ins, (keep_ref, send_ref) = refs[:n_in], refs[n_in:]
    rows, D = idx_ref.shape[0], ins[plan[0][0]].shape[1]
    take = (lax.broadcasted_iota(jnp.int32, (rows, D), 1) == idx_ref[...]).astype(F32).astype(BF)
    at = 0
    for a_at, grads in plan:
        aT = jnp.concatenate([nt(take, ins[a_at][...]), nt(take, ins[a_at + 1][...])], 1).astype(BF)
        for d_at in grads:
            width = ins[d_at].shape[1]
            step = 384 if width % 384 == 0 else 128
            for c in range(0, width, step):
                sl = slice(c, c + step)
                both = jnp.concatenate([ins[d_at][:, sl], ins[d_at + 1][:, sl]], 0)
                got = nn(aT, both)
                keep_ref[:, at : at + step] = got[: rows // 2].astype(BF)
                send_ref[:, at : at + step] = got[rows // 2 :].astype(BF)
                at += step


def weight_grads(idx, terms):
    ins, plan, width, flops = [], [], 0, 0
    for a, grads in terms:
        at = len(ins)
        ins += list(a)
        ds = []
        for d in grads:
            ds.append(len(ins))
            ins += list(d)
            width += d[0].shape[1]
            flops += 4 * d[0].shape[0] * d[0].shape[1] * idx.shape[0]
        plan.append((at, ds))
    half = idx.shape[0] // 2
    return whole(
        functools.partial(weight_body, plan, len(ins)),
        "weight_grads",
        [((half, width), BF)] * 2,
        idx,
        *ins,
        flops=flops,
    )


def swap(x, bit, n):
    return lax.ppermute(x, "blk", [(i, i ^ bit) for i in range(n)])


def other_tp(x):
    return lax.ppermute(x, "tp", [(0, 1), (1, 0)])


def scatter_sum(keep, send, n):
    total = keep.astype(F32) + swap(send, 2, n).astype(F32)
    total = total.reshape(4, n // 16, -1, total.shape[1])
    low = total.astype(BF)
    total = total[0]
    for k in range(1, 4):
        total = total + swap(low[k], 4 * k, n).astype(F32)
    bit = n // 2
    while total.shape[0] > 1:
        half = total.shape[0] // 2
        total = total[:half] + swap(total[half:].astype(BF), bit, n).astype(F32)
        bit //= 2
    return total[0]


def on_device(
    n,
    encoder_in,
    decoder_in,
    lengths,
    retrieved,
    band_start,
    cotangent,
    enc_query,
    enc_key,
    enc_value,
    enc_mix,
    attn_gain,
    attn_shift,
    enc_up,
    enc_down,
    ffn_gain,
    ffn_shift,
    self_query,
    self_key,
    self_value,
    self_mix,
    self_gain,
    self_shift,
    cross_query,
    cross_key,
    cross_value,
    cross_mix,
    cross_gain,
    cross_shift,
    dec_up,
    dec_down,
    last_gain,
    last_shift,
):
    group_rows, D = encoder_in.shape
    C = cross_query.shape[1]
    FF = enc_up.shape[1]
    hi = n // 16
    me = lax.axis_index("blk")
    core = lambda x: swap(x, 1, n)
    par = jnp.stack(
        [attn_gain, attn_shift, ffn_gain, ffn_shift, self_gain, self_shift, cross_gain, cross_shift, last_gain, last_shift]
    )

    share = D // n
    t = jnp.arange(D // 2, dtype=jnp.int32)
    block = t // share
    rel = 2 * (block // (n // 4)) + 4 * ((block // hi) % 4) + 16 * (block % hi)
    idx = ((me ^ rel) * share + t % share).reshape(D // 2, 1)

    xe = (encoder_in, core(encoder_in))
    xd = (decoder_in, core(decoder_in))
    *enc_kept, enc_o, enc_part = attend_fwd(encoder_in, enc_query, enc_key, enc_value, enc_mix)
    enc_other = other_tp(enc_part)
    *self_kept, self_o, self_part = attend_fwd(decoder_in, self_query, self_key, self_value, self_mix, lengths)
    self_other = other_tp(self_part)
    chosen = picks(retrieved, band_start, n, group_rows // 2)

    v1, u1, low1, act1, gp1, part1 = ffn_fwd(0, encoder_in, enc_part, enc_other, par, enc_up, enc_down)
    other1 = other_tp(part1)
    vd, ud, lowd, qc = cross_q(4, decoder_in, self_part, self_other, par, cross_query)
    v2, encoded, enc_low, store = store_fwd(2, u1, part1, other1, par, cross_key, cross_value)

    store = store[None]
    for b in range(4, n.bit_length() - 1):
        store = jnp.concatenate([store, swap(store, 1 << b, n)], 0)
    pieces = []
    gids = []
    for k in range(4):
        z = store if k == 0 else swap(store, 4 * k, n)
        y = swap(z, 2, n)
        pieces.append((z, y, core(z), core(y)))
        rel = [16 * h + 4 * k + r for h in range(hi) for r in (0, 2, 1, 3)]
        gids.append(me ^ jnp.array(rel, jnp.int32))
    state = None
    for k in range(4):
        state = cross_fwd(gids[k], qc, pieces[k], chosen, state)
    log_total, of, oc, partc = cross_mix_fwd(*state, cross_mix)
    otherc = other_tp(partc)
    vc, uc, lowc, actc, gpc, part3 = ffn_fwd(6, ud, partc, otherc, par, dec_up, dec_down)
    other3 = other_tp(part3)
    decoded, dlast, dlast_low, dhd, gg_last, part4 = last_fwd_back(
        8, uc, part3, other3, cotangent, par, gpc, dec_up, dec_down
    )
    other4 = other_tp(part4)
    dcross, dcross_low, do, delta, gg_cross = cross_mix_back(6, dlast, part4, other4, vc, par, of, cross_mix)

    both = lambda x: (x, core(x))
    first_sum = scatter_sum(
        *weight_grads(
            idx,
            [
                (both(dlast_low), [both(actc)]),
                (both(lowc), [both(dhd)]),
                (both(dcross_low), [both(oc)]),
            ],
        ),
        n,
    )

    dq = None
    terms = []
    for k in (3, 2, 1, 0):
        dq, keep, send = cross_back(gids[k], qc, do, log_total, delta, pieces[k], chosen, dq)
        got = core(send)
        mine = (keep[:, 0].astype(F32) + got[:, 0].astype(F32)).astype(BF)
        away = (keep[:, 1].astype(F32) + got[:, 1].astype(F32)).astype(BF)
        mine = (mine.astype(F32) + swap(away, 2, n).astype(F32)).astype(BF)
        terms.append(mine if k == 0 else swap(mine, 4 * k, n))
    bit = n // 2
    while terms[0].shape[0] > 1:
        half = terms[0].shape[0] // 2
        total = functools.reduce(lambda x, y: x + y, [t.astype(F32) for t in terms])
        terms = [total[:half].astype(BF), swap(total[half:].astype(BF), bit, n)]
        bit //= 2
    dqc, partq = cross_q_back(dq, cross_query)
    otherq = other_tp(partq)
    dkv, part5 = store_back(terms, cross_key, cross_value)
    other5 = other_tp(part5)

    dself, dself_low, dqkvd, gg_self, part6 = attend_back(
        4, dcross, partq, otherq, vd, par, self_kept, (self_query, self_key, self_value, self_mix), lengths
    )
    other6 = other_tp(part6)
    grad_decoder_in = dself + (part6.astype(F32) + other6.astype(F32))
    second_sum = scatter_sum(
        *weight_grads(
            idx,
            [
                (both(lowd), [both(dqc)]),
                (xd, [both(dqkvd)]),
                (both(dself_low), [both(self_o)]),
                (both(enc_low), [both(dkv)]),
            ],
        ),
        n,
    )

    dffn, dffn_low, dhe, gg_ffn, part7 = ffn_back(2, part5, other5, v2, par, gp1, enc_up, enc_down)
    other7 = other_tp(part7)
    third_sum = scatter_sum(
        *weight_grads(idx, [(both(dffn_low), [both(act1)]), (both(low1), [both(dhe)])]),
        n,
    )
    dattn, dattn_low, dqkve, gg_attn, part8 = attend_back(
        0, dffn, part7, other7, v1, par, enc_kept, (enc_query, enc_key, enc_value, enc_mix)
    )
    other8 = other_tp(part8)
    grad_encoder_in = dattn + (part8.astype(F32) + other8.astype(F32))

    gains = jnp.concatenate([g[:2] for g in (gg_attn, gg_ffn, gg_self, gg_cross, gg_last)])
    gains = jnp.pad(gains.astype(BF), ((0, 6), (0, 0)))
    gains = (gains.astype(F32) + core(gains).astype(F32)).astype(BF)
    lanes = jnp.eye(16, 128, dtype=BF)
    keep, send = weight_grads(
        idx, [(xe, [both(dqkve)]), (both(dattn_low), [both(enc_o)]), ((gains, jnp.zeros_like(gains)), [(lanes, lanes)])]
    )
    fourth_sum = scatter_sum(keep, send, n)

    cut = lambda total, at, width: total[:, at : at + width]
    gain_of = [fourth_sum[:, 4 * C + i] for i in range(10)]
    return (
        encoded,
        decoded,
        grad_encoder_in,
        grad_decoder_in,
        cut(fourth_sum, 0, C),
        cut(fourth_sum, C, C),
        cut(fourth_sum, 2 * C, C),
        cut(fourth_sum, 3 * C, C).T,
        gain_of[0],
        gain_of[1],
        cut(third_sum, FF, FF),
        cut(third_sum, 0, FF).T,
        gain_of[2],
        gain_of[3],
        cut(second_sum, C, C),
        cut(second_sum, 2 * C, C),
        cut(second_sum, 3 * C, C),
        cut(second_sum, 4 * C, C).T,
        gain_of[4],
        gain_of[5],
        cut(second_sum, 0, C),
        cut(second_sum, 5 * C, C),
        cut(second_sum, 6 * C, C),
        cut(first_sum, 2 * FF, C).T,
        gain_of[6],
        gain_of[7],
        cut(first_sum, FF, FF),
        cut(first_sum, 0, FF).T,
        gain_of[8],
        gain_of[9],
    )


def solution(mesh):
    rows, both, cols, down = P("blk", None), P("blk", "tp"), P(None, "tp"), P("tp", None)
    attn = (cols, cols, cols, down, P(), P())
    ffn = (cols, down, P(), P())
    in_specs = (rows, rows, P("blk"), P("blk", "tp", None), both, rows) + attn + ffn + attn + attn + ffn
    mixed = P("tp", "blk")
    grad_attn = (both, both, both, mixed, P("blk"), P("blk"))
    grad_ffn = (both, mixed, P("blk"), P("blk"))
    out_specs = (rows,) * 4 + grad_attn + grad_ffn + grad_attn + grad_attn + grad_ffn
    return jax.shard_map(
        functools.partial(on_device, mesh.shape["blk"]),
        mesh=mesh,
        in_specs=in_specs,
        out_specs=out_specs,
        check_vma=False,
    )
```

time: 1740 us -> 452 us (0.26)
  waiting for transfers between devices: 1330 us -> 229 us
  matrix products: 161 us -> 0 us
  Pallas kernels: 0 us -> 97 us
  blocking collectives: 62 us -> 0 us
  starting transfers between devices: 2.19 us -> 64 us
  local copies, waits for them, and re-layouts: 97.8 us -> 36 us
  other arithmetic: 60.2 us -> 16.1 us
    reduce_scatter x11 -> x0, waiting for transfers between devices: 720 us -> none  [the longest x1 135 us: on_device(): lax.psum_scatter(grad_store, 'blk', scatter_dimension=1, tiled=True)]
    unnamed x32 -> x0, waiting for transfers between devices: 368 us -> none
    ppermute x0 -> x76, waiting for transfers between devices: none -> 229 us  [the longest x65 185 us: swap(): return lax.ppermute(x, 'blk', [(i, i ^ bit) for i in range(n)])]
    psum x8 -> x0, waiting for transfers between devices: 206 us -> none  [head_sum(): return lax.psum(partial_value, 'tp')]
    dot_general x65 -> x0, matrix products: 157 us -> none  [the longest x16 42.8 us: outer(): lax.dot_general(inputs, grads, (((0,), (0,)), ((), ())), preferred_elemen...]
    pallas_call x0 -> x27, Pallas kernels: none -> 97 us  [the longest x18 46.9 us: whole(): pl.pallas_call(body, name=name, out_shape=[jax.ShapeDtypeStruct(s, d) for...]
    ppermute x0 -> x76, starting transfers between devices: none -> 64 us  [the longest x65 49.4 us: swap(): return lax.ppermute(x, 'blk', [(i, i ^ bit) for i in range(n)])]
    unnamed x1 -> x0, blocking collectives: 62 us -> none
  transfers between devices with their start and end apart: 26 -> 76, of which waited for: 24 -> 29; matrix products, arithmetic and copies ran while one was open for 8% -> 6% of each run, Pallas kernels for 0% -> 16%
where the time goes in v1:
time: 452 us; the launch traced here: 445 us
  waiting for transfers between devices  229 us (51%)
  Pallas kernels  97 us (21%)
  starting transfers between devices  64 us (14%)
  local copies, waits for them, and re-layouts  36 us (8%)
  other arithmetic  16.1 us (4%)
    ppermute x65, waiting for transfers between devices, swap(): return lax.ppermute(x, 'blk', [(i, i ^ bit) for i in range(n)])  185 us
    ppermute x65, starting transfers between devices, swap(): return lax.ppermute(x, 'blk', [(i, i ^ bit) for i in range(n)])  49.4 us
    pallas_call x18, Pallas kernels, whole(): pl.pallas_call(body, name=name, out_shape=[jax.ShapeDtypeStruct(s, d) for...  46.9 us
    ppermute x11, waiting for transfers between devices, other_tp(): return lax.ppermute(x, 'tp', [(0, 1), (1, 0)])  43.5 us
    unnamed x205, local copies, waits for them, and re-layouts  28.9 us
    pallas_call x4, Pallas kernels, cross_back(): pl.pallas_call(functools.partial(cross_back_body, first), name='cross_bac...  25.6 us
    pallas_call x4, Pallas kernels, cross_fwd(): pl.pallas_call(functools.partial(cross_fwd_body, first), name='cross_fwd'...  16.5 us
    ppermute x11, starting transfers between devices, other_tp(): return lax.ppermute(x, 'tp', [(0, 1), (1, 0)])  14.7 us
  transfers between devices with their start and end apart: 76, of which 29 were waited for; matrix products, arithmetic and copies ran while one was open for 6% of the time, Pallas kernels for 16%

profile of v1, /device:TPU:0, one launch (start us, length us, event | category | flops | bytes accessed | tf_op | source)
XLA Modules:
  0.0 445.0 jit_solution(4326262198994262239)
XLA Ops:
  15.0 9.1 %collective-permute-done.oth = bf16[256,768]{1,0:T(8,128)(2,1)} collective-permute-done((bf16[256,768]{1,0:T(8,128)(2,1)}, bf16[256,768]{1,0:T(8,128)(2,1)}, u32[]{:S(2)}, u32[]{:S(2)}) %collective-permute-start) | collective-permute-done | bytes 393248 | tf_op jit(solution)/shard_map/ppermute | solution.py:665
  24.0 4.7 %ffn_fwd.2 = (f32[256,768]{1,0:T(8,128)S(1)}, f32[256,768]{1,0:T(8,128)S(1)}, bf16[256,768]{1,0:T(8,128)(2,1)}, bf16[256,1536]{1,0:T(8,128)(2,1)S(1)}, bf16[256,...) custom-call(bf16[256,768]{1,0:T(8,128)(2,1)S(1)} %copy-done.12, bf16[256,768]{1,0:T(8,128)(2,1)} %get-tuple-element.126.own, ...), custom_call_target="tpu_custom_call" | custom-call | flops 1207959552 | bytes 9845760 | tf_op jit(solution)/shard_map/ffn_fwd/pallas_call | solution.py:36
  36.0 7.5 %collective-permute-done.1.oth = bf16[256,768]{1,0:T(8,128)(2,1)S(1)} collective-permute-done((bf16[256,768]{1,0:T(8,128)(2,1)S(1)}, bf16[256,768]{1,0:T(8,128)(2,1)S(1)}, u32[]{:S(2)}, u32[]{:S(2)}) %collective-permute-start.1) | collective-permute-done | bytes 393248 | tf_op jit(solution)/shard_map/ppermute | solution.py:665
  53.7 7.6 %collective-permute-done.11.refs_0_ = bf16[1,2,256,384]{3,2,1,0:T(8,128)(2,1)} collective-permute-done((bf16[1,2,256,384]{3,2,1,0:T(8,128)(2,1)}, bf16[1,2,256,384]{3,2,1,0:T(8,128)(2,1)}, u32[]{:S(2)}, u32[]{:S(2)}) %collective-permute-start.11) | collective-permute-done | bytes 393248 | tf_op jit(solution)/shard_map/ppermute | solution.py:661
  63.1 6.1 %collective-permute-done.3.refs_0_ = bf16[1,2,256,384]{3,2,1,0:T(8,128)(2,1)} collective-permute-done((bf16[1,2,256,384]{3,2,1,0:T(8,128)(2,1)}, bf16[1,2,256,384]{3,2,1,0:T(8,128)(2,1)}, u32[]{:S(2)}, u32[]{:S(2)}) %collective-permute-start.3) | collective-permute-done | bytes 393248 | tf_op jit(solution)/shard_map/ppermute | solution.py:661
  69.2 12.8 %collective-permute-done.7.refs_0_ = bf16[1,2,256,384]{3,2,1,0:T(8,128)(2,1)} collective-permute-done((bf16[1,2,256,384]{3,2,1,0:T(8,128)(2,1)}, bf16[1,2,256,384]{3,2,1,0:T(8,128)(2,1)}, u32[]{:S(2)}, u32[]{:S(2)}) %collective-permute-start.7) | collective-permute-done | bytes 393248 | tf_op jit(solution)/shard_map/ppermute | solution.py:661
  93.2 4.2 collective-permute-done.8.refs_1_
  98.4 8.0 %picks.1.refs_4_.refs_5_.refs_6_.refs_7_ = f32[16,3,128,256]{3,2,1,0:T(8,128)} custom-call(f32[6,1024,128]{2,1,0:T(8,128)S(1)} %convert_bitcast_fusion.pick_ref, s32[6,128]{1,0:T(8,128)S(1)} %bitcast.114), custom_call_target="tpu_custom_call" | custom-call | tf_op jit(solution)/shard_map/picks/pallas_call | solution.py:244
  107.0 4.2 cross_fwd.4
  111.2 4.1 cross_fwd.5
  119.3 4.3 cross_fwd.7
  125.5 5.4 %collective-permute-done.18.oth = bf16[128,768]{1,0:T(8,128)(2,1)S(1)} collective-permute-done((bf16[128,768]{1,0:T(8,128)(2,1)S(1)}, bf16[128,768]{1,0:T(8,128)(2,1)S(1)}, u32[]{:S(2)}, u32[]{:S(2)}) %collective-permute-start.18) | collective-permute-done | bytes 196640 | tf_op jit(solution)/shard_map/ppermute | solution.py:665
  135.4 4.5 %collective-permute-done.19.oth = bf16[128,768]{1,0:T(8,128)(2,1)S(1)} collective-permute-done((bf16[128,768]{1,0:T(8,128)(2,1)S(1)}, bf16[128,768]{1,0:T(8,128)(2,1)S(1)}, u32[]{:S(2)}, u32[]{:S(2)}) %collective-permute-start.19) | collective-permute-done | bytes 196640 | tf_op jit(solution)/shard_map/ppermute | solution.py:665
  145.1 4.1 collective-permute-done.20.oth
  150.8 6.6 %cross_back.4 = (f32[3,128,256]{2,1,0:T(8,128)S(1)}, bf16[1,2,2,256,384]{4,3,2,1,0:T(8,128)(2,1)S(1)}, bf16[1,2,2,256,384]{4,3,2,1,0:T(8,128)(2,1)}) custom-call(s32[4]{0:T(128)S(1)} %broadcast_xor_fusion.3.gid_ref, bf16[128,384]{1,0:T(8,128)(2,1)S(1)} %get-tuple-element.132.q_ref, bf16[128,384]{1,0:T(8,128)(2,1)S(1)} %get-tuple-element.155.do_ref, ...), custom_call_target="tpu_custom_call" | custom-call | flops 1006632960 | bytes 3145728 | tf_op jit(solution)/shard_map/cross_back/pallas_call | solution.py:522
  158.5 6.5 %cross_back.5 = (f32[3,128,256]{2,1,0:T(8,128)S(1)}, bf16[1,2,2,256,384]{4,3,2,1,0:T(8,128)(2,1)S(1)}, bf16[1,2,2,256,384]{4,3,2,1,0:T(8,128)(2,1)}) custom-call(s32[4]{0:T(128)S(1)} %broadcast_xor_fusion.2.gid_ref, bf16[128,384]{1,0:T(8,128)(2,1)S(1)} %get-tuple-element.132.q_ref, bf16[128,384]{1,0:T(8,128)(2,1)S(1)} %get-tuple-element.155.do_ref, ...), custom_call_target="tpu_custom_call" | custom-call | flops 1006632960 | bytes 3145728 | tf_op jit(solution)/shard_map/cross_back/pallas_call | solution.py:522
  165.6 6.6 %cross_back.6 = (f32[3,128,256]{2,1,0:T(8,128)S(1)}, bf16[1,2,2,256,384]{4,3,2,1,0:T(8,128)(2,1)S(1)}, bf16[1,2,2,256,384]{4,3,2,1,0:T(8,128)(2,1)}) custom-call(s32[4]{0:T(128)S(1)} %broadcast_xor_fusion.1.gid_ref, bf16[128,384]{1,0:T(8,128)(2,1)S(1)} %get-tuple-element.132.q_ref, bf16[128,384]{1,0:T(8,128)(2,1)S(1)} %get-tuple-element.155.do_ref, ...), custom_call_target="tpu_custom_call" | custom-call | flops 1006632960 | bytes 3145728 | tf_op jit(solution)/shard_map/cross_back/pallas_call | solution.py:522
  172.2 5.9 %cross_back.7 = (f32[3,128,256]{2,1,0:T(8,128)S(1)}, bf16[1,2,2,256,384]{4,3,2,1,0:T(8,128)(2,1)S(1)}, bf16[1,2,2,256,384]{4,3,2,1,0:T(8,128)(2,1)S(1)}) custom-call(s32[4]{0:T(128)S(1)} %broadcast_xor_fusion.gid_ref, bf16[128,384]{1,0:T(8,128)(2,1)S(1)} %get-tuple-element.132.q_ref, bf16[128,384]{1,0:T(8,128)(2,1)S(1)} %get-tuple-element.155.do_ref, ...), custom_call_target="tpu_custom_call" | custom-call | flops 1006632960 | bytes 3145728 | tf_op jit(solution)/shard_map/cross_back/pallas_call | solution.py:522
  202.3 34.4 %collective-permute-done.22 = bf16[1,2,256,384]{3,2,1,0:T(8,128)(2,1)S(1)} collective-permute-done((bf16[1,2,256,384]{3,2,1,0:T(8,128)(2,1)S(1)}, bf16[1,2,256,384]{3,2,1,0:T(8,128)(2,1)S(1)}, u32[]{:S(2)}, u32[]{:S(2)}) %collective-permute-start.22) | collective-permute-done | bytes 393248 | tf_op jit(solution)/shard_map/ppermute | solution.py:661
  239.3 5.8 %collective-permute-done.25 = bf16[1,2,256,384]{3,2,1,0:T(8,128)(2,1)S(1)} collective-permute-done((bf16[1,2,256,384]{3,2,1,0:T(8,128)(2,1)S(1)}, bf16[1,2,256,384]{3,2,1,0:T(8,128)(2,1)S(1)}, u32[]{:S(2)}, u32[]{:S(2)}) %collective-permute-start.25) | collective-permute-done | bytes 393248 | tf_op jit(solution)/shard_map/ppermute | solution.py:661
  247.7 5.8 %collective-permute-done.28 = bf16[1,2,256,384]{3,2,1,0:T(8,128)(2,1)S(1)} collective-permute-done((bf16[1,2,256,384]{3,2,1,0:T(8,128)(2,1)S(1)}, bf16[1,2,256,384]{3,2,1,0:T(8,128)(2,1)S(1)}, u32[]{:S(2)}, u32[]{:S(2)}) %collective-permute-start.28) | collective-permute-done | bytes 393248 | tf_op jit(solution)/shard_map/ppermute | solution.py:661
  267.6 21.9 %collective-permute-done.26.refs_1_ = bf16[1,2,256,384]{3,2,1,0:T(8,128)(2,1)S(1)} collective-permute-done((bf16[1,2,256,384]{3,2,1,0:T(8,128)(2,1)S(1)}, bf16[1,2,256,384]{3,2,1,0:T(8,128)(2,1)S(1)}, u32[]{:S(2)}, u32[]{:S(2)}) %collective-permute-start.26) | collective-permute-done | bytes 393248 | tf_op jit(solution)/shard_map/ppermute | solution.py:661
  297.4 6.3 %collective-permute-done.32.oth = bf16[256,768]{1,0:T(8,128)(2,1)S(1)} collective-permute-done((bf16[256,768]{1,0:T(8,128)(2,1)S(1)}, bf16[256,768]{1,0:T(8,128)(2,1)S(1)}, u32[]{:S(2)}, u32[]{:S(2)}) %collective-permute-start.32) | collective-permute-done | bytes 393248 | tf_op jit(solution)/shard_map/ppermute | solution.py:665
  304.5 4.9 %ffn_back.1 = (f32[256,768]{1,0:T(8,128)S(1)}, bf16[256,768]{1,0:T(8,128)(2,1)S(1)}, bf16[256,1536]{1,0:T(8,128)(2,1)}, f32[8,768]{1,0:T(8,128)S(1)}, bf16[256,768]{1,0:T(8,128)(2,1)S(1)}) custom-call(bf16[256,768]{1,0:T(8,128)(2,1)S(1)} %get-tuple-element.169.own, bf16[256,768]{1,0:T(8,128)(2,1)S(1)} %collective-permute-done.32.oth, ...), custom_call_target="tpu_custom_call" | custom-call | flops 1207959552 | bytes 9477120 | tf_op jit(solution)/shard_map/ffn_back/pallas_call | solution.py:36
  310.0 12.9 %collective-permute-done.74 = bf16[1,48,3456]{2,1,0:T(8,128)(2,1)S(1)} collective-permute-done((bf16[1,48,3456]{2,1,0:T(8,128)(2,1)S(1)}, bf16[1,48,3456]{2,1,0:T(8,128)(2,1)S(1)}, u32[]{:S(2)}, u32[]{:S(2)}) %collective-permute-start.74) | collective-permute-done | bytes 331808 | tf_op jit(solution)/shard_map/ppermute | solution.py:661
  334.5 5.2 %attend_back.2 = (f32[256,768]{1,0:T(8,128)S(1)}, bf16[256,768]{1,0:T(8,128)(2,1)S(1)}, bf16[256,1152]{1,0:T(8,128)(2,1)S(1)}, f32[8,768]{1,0:T(8,128)S(1)}, bf16[256,768]{1,0:T(8,128)(2,1)S(1)}) custom-call(f32[256,768]{1,0:T(8,128)} %copy-done.21, bf16[256,768]{1,0:T(8,128)(2,1)S(1)} %get-tuple-element.173.refs_1_, ...), custom_call_target="tpu_custom_call" | custom-call | flops 1107296256 | bytes 7511040 | tf_op jit(solution)/shard_map/attend_back/pallas_call | solution.py:36
  348.4 5.5 %weight_grads.5 = (bf16[192,3072]{1,0:T(8,128)(2,1)S(1)}, bf16[192,3072]{1,0:T(8,128)(2,1)}) custom-call(s32[384,1]{1,0:T(8,128)S(1)} %fusion.38.idx_ref, bf16[256,768]{1,0:T(8,128)(2,1)S(1)} %copy-done.33, bf16[256,768]{1,0:T(8,128)(2,1)S(1)} %collective-permute-done.46.refs_1_, bf16[256,1536]{1,0:T(8,128)(2,1)S(1)} %copy-done.15, ...), custom_call_target="tpu_custom_call" | custom-call | flops 1207959552 | bytes 7079424 | tf_op jit(solution)/shard_map/weight_grads/pallas_call | solution.py:36
  367.1 12.6 %collective-permute-done.64 = bf16[1,48,2688]{2,1,0:T(8,128)(2,1)S(1)} collective-permute-done((bf16[1,48,2688]{2,1,0:T(8,128)(2,1)S(1)}, bf16[1,48,2688]{2,1,0:T(8,128)(2,1)S(1)}, u32[]{:S(2)}, u32[]{:S(2)}) %collective-permute-start.64) | collective-permute-done | bytes 258080 | tf_op jit(solution)/shard_map/ppermute | solution.py:661
  379.9 22.9 %collective-permute-done.42 = bf16[192,1664]{1,0:T(8,128)(2,1)S(1)} collective-permute-done((bf16[192,1664]{1,0:T(8,128)(2,1)S(1)}, bf16[192,1664]{1,0:T(8,128)(2,1)S(1)}, u32[]{:S(2)}, u32[]{:S(2)}) %collective-permute-start.42) | collective-permute-done | bytes 639008 | tf_op jit(solution)/shard_map/ppermute | solution.py:661
  411.9 6.3 %collective-permute-done.44 = bf16[1,48,1664]{2,1,0:T(8,128)(2,1)S(1)} collective-permute-done((bf16[1,48,1664]{2,1,0:T(8,128)(2,1)S(1)}, bf16[1,48,1664]{2,1,0:T(8,128)(2,1)S(1)}, u32[]{:S(2)}, u32[]{:S(2)}) %collective-permute-start.44) | collective-permute-done | bytes 159776 | tf_op jit(solution)/shard_map/ppermute | solution.py:661
  424.8 5.9 %collective-permute-done.53 = bf16[1,48,3072]{2,1,0:T(8,128)(2,1)S(1)} collective-permute-done((bf16[1,48,3072]{2,1,0:T(8,128)(2,1)S(1)}, bf16[1,48,3072]{2,1,0:T(8,128)(2,1)S(1)}, u32[]{:S(2)}, u32[]{:S(2)}) %collective-permute-start.53) | collective-permute-done | bytes 294944 | tf_op jit(solution)/shard_map/ppermute | solution.py:661
  430.7 12.9 %collective-permute-done.52 = bf16[1,48,3072]{2,1,0:T(8,128)(2,1)S(1)} collective-permute-done((bf16[1,48,3072]{2,1,0:T(8,128)(2,1)S(1)}, bf16[1,48,3072]{2,1,0:T(8,128)(2,1)S(1)}, u32[]{:S(2)}, u32[]{:S(2)}) %collective-permute-start.52) | collective-permute-done | bytes 294944 | tf_op jit(solution)/shard_map/ppermute | solution.py:661
  (407 shorter events, 166.6 us)
Async XLA Ops:
  48.8 20.4 %collective-permute-start.3 = (bf16[1,2,256,384]{3,2,1,0:T(8,128)(2,1)}, bf16[1,2,256,384]{3,2,1,0:T(8,128)(2,1)}, u32[]{:S(2)}, u32[]{:S(2)}) collective-permute-start(bf16[1,2,256,384]{3,2,1,0:T(8,128)(2,1)} %bitcast.refs_0_), channel_id=1, source_target_pairs={{0,24},{2,26},{4,28},{6,30},{8,16},{10,18},{12,20},{14,22},{16,8},... | collective-permute-start | bytes 1179656 | tf_op jit(solution)/shard_map/ppermute | solution.py:661
  51.3 30.7 %collective-permute-start.7 = (bf16[1,2,256,384]{3,2,1,0:T(8,128)(2,1)}, bf16[1,2,256,384]{3,2,1,0:T(8,128)(2,1)}, u32[]{:S(2)}, u32[]{:S(2)}) collective-permute-start(bf16[1,2,256,384]{3,2,1,0:T(8,128)(2,1)} %bitcast.refs_0_), channel_id=1, source_target_pairs={{0,16},{2,18},{4,20},{6,22},{8,24},{10,26},{12,28},{14,30},{16,0},... | collective-permute-start | bytes 1179656 | tf_op jit(solution)/shard_map/ppermute | solution.py:661
  51.4 32.1 %collective-permute-start.15 = (bf16[1,2,256,384]{3,2,1,0:T(8,128)(2,1)}, bf16[1,2,256,384]{3,2,1,0:T(8,128)(2,1)}, u32[]{:S(2)}, u32[]{:S(2)}) collective-permute-start(bf16[1,2,256,384]{3,2,1,0:T(8,128)(2,1)} %bitcast.refs_0_), channel_id=1, source_target_pairs={{0,4},{2,6},{4,0},{6,2},{8,12},{10,14},{12,8},{14,10},{16,20},{18,... | collective-permute-start | bytes 1179656 | tf_op jit(solution)/shard_map/ppermute | solution.py:661
  53.6 30.4 %collective-permute-start.16 = (bf16[1,2,256,384]{3,2,1,0:T(8,128)(2,1)}, bf16[1,2,256,384]{3,2,1,0:T(8,128)(2,1)}, u32[]{:S(2)}, u32[]{:S(2)}) collective-permute-start(bf16[1,2,256,384]{3,2,1,0:T(8,128)(2,1)} %bitcast.refs_0_), channel_id=1, source_target_pairs={{0,2},{2,0},{4,6},{6,4},{8,10},{10,8},{12,14},{14,12},{16,18},{18,... | collective-permute-start | bytes 1179656 | tf_op jit(solution)/shard_map/ppermute | solution.py:661
  61.2 36.1 %collective-permute-start.12 = (bf16[1,2,256,384]{3,2,1,0:T(8,128)(2,1)}, bf16[1,2,256,384]{3,2,1,0:T(8,128)(2,1)}, u32[]{:S(2)}, u32[]{:S(2)}) collective-permute-start(bf16[1,2,256,384]{3,2,1,0:T(8,128)(2,1)} %collective-permute-done.11.refs_0_), channel_id=1, source_target_pairs={{0,4},{2,6},{4,0},{6,2},{8,12},{10,14},{12,8},{14,10},{16,20},{18,... | collective-permute-start | bytes 1179656 | tf_op jit(solution)/shard_map/ppermute | solution.py:661
  69.2 28.7 %collective-permute-start.13 = (bf16[1,2,256,384]{3,2,1,0:T(8,128)(2,1)}, bf16[1,2,256,384]{3,2,1,0:T(8,128)(2,1)}, u32[]{:S(2)}, u32[]{:S(2)}) collective-permute-start(bf16[1,2,256,384]{3,2,1,0:T(8,128)(2,1)} %collective-permute-done.11.refs_0_), channel_id=1, source_target_pairs={{0,2},{2,0},{4,6},{6,4},{8,10},{10,8},{12,14},{14,12},{16,18},{18,... | collective-permute-start | bytes 1179656 | tf_op jit(solution)/shard_map/ppermute | solution.py:661
  93.2 26.1 %collective-permute-start.5 = (bf16[1,2,256,384]{3,2,1,0:T(8,128)(2,1)}, bf16[1,2,256,384]{3,2,1,0:T(8,128)(2,1)S(1)}, u32[]{:S(2)}, u32[]{:S(2)}) collective-permute-start(bf16[1,2,256,384]{3,2,1,0:T(8,128)(2,1)} %collective-permute-done.3.refs_0_), channel_id=1, source_target_pairs={{0,2},{2,0},{4,6},{6,4},{8,10},{10,8},{12,14},{14,12},{16,18},{18,... | collective-permute-start | bytes 1179656 | tf_op jit(solution)/shard_map/ppermute | solution.py:661
  97.4 21.9 %collective-permute-start.6 = (bf16[1,2,256,384]{3,2,1,0:T(8,128)(2,1)}, bf16[1,2,256,384]{3,2,1,0:T(8,128)(2,1)S(1)}, u32[]{:S(2)}, u32[]{:S(2)}) collective-permute-start(bf16[1,2,256,384]{3,2,1,0:T(8,128)(2,1)} %collective-permute-done.4.refs_1_), channel_id=1, source_target_pairs={{0,2},{2,0},{4,6},{6,4},{8,10},{10,8},{12,14},{14,12},{16,18},{18,... | collective-permute-start | bytes 1179656 | tf_op jit(solution)/shard_map/ppermute | solution.py:661
  157.4 37.5 %collective-permute-start.21 = (bf16[1,2,2,256,384]{4,3,2,1,0:T(8,128)(2,1)}, bf16[1,2,2,256,384]{4,3,2,1,0:T(8,128)(2,1)}, u32[]{:S(2)}, u32[]{:S(2)}) collective-permute-start(bf16[1,2,2,256,384]{4,3,2,1,0:T(8,128)(2,1)} %get-tuple-element.159), channel_id=1, source_target_pairs={{0,2},{2,0},{4,6},{6,4},{8,10},{10,8},{12,14},{14,12},{16,18},{18,... | collective-permute-start | bytes 2359304 | tf_op jit(solution)/shard_map/ppermute | solution.py:661
  157.4 21.7 %collective-permute-start.67 = (bf16[128,1536]{1,0:T(8,128)(2,1)S(1)}, bf16[128,1536]{1,0:T(8,128)(2,1)S(1)}, u32[]{:S(2)}, u32[]{:S(2)}) collective-permute-start(bf16[128,1536]{1,0:T(8,128)(2,1)S(1)} %get-tuple-element.215.refs_2_), channel_id=1, source_target_pairs={{0,2},{2,0},{4,6},{6,4},{8,10},{10,8},{12,14},{14,12},{16,18},{18,... | collective-permute-start | bytes 1179656 | tf_op jit(solution)/shard_map/ppermute | solution.py:661
  158.0 24.6 %collective-permute-start.69 = (bf16[128,1536]{1,0:T(8,128)(2,1)S(1)}, bf16[128,1536]{1,0:T(8,128)(2,1)S(1)}, u32[]{:S(2)}, u32[]{:S(2)}) collective-permute-start(bf16[128,1536]{1,0:T(8,128)(2,1)S(1)} %get-tuple-element.217.refs_6_), channel_id=1, source_target_pairs={{0,2},{2,0},{4,6},{6,4},{8,10},{10,8},{12,14},{14,12},{16,18},{18,... | collective-permute-start | bytes 1179656 | tf_op jit(solution)/shard_map/ppermute | solution.py:661
  165.0 31.2 %collective-permute-start.24 = (bf16[1,2,2,256,384]{4,3,2,1,0:T(8,128)(2,1)}, bf16[1,2,2,256,384]{4,3,2,1,0:T(8,128)(2,1)}, u32[]{:S(2)}, u32[]{:S(2)}) collective-permute-start(bf16[1,2,2,256,384]{4,3,2,1,0:T(8,128)(2,1)} %get-tuple-element.162), channel_id=1, source_target_pairs={{0,2},{2,0},{4,6},{6,4},{8,10},{10,8},{12,14},{14,12},{16,18},{18,... | collective-permute-start | bytes 2359304 | tf_op jit(solution)/shard_map/ppermute | solution.py:661
  184.8 108.0 %collective-permute-start.56 = (bf16[128,768]{1,0:T(8,128)(2,1)S(1)}, bf16[128,768]{1,0:T(8,128)(2,1)S(1)}, u32[]{:S(2)}, u32[]{:S(2)}) collective-permute-start(bf16[128,768]{1,0:T(8,128)(2,1)S(1)} %copy-done.10), channel_id=1, source_target_pairs={{0,2},{2,0},{4,6},{6,4},{8,10},{10,8},{12,14},{14,12},{16,18},{18,... | collective-permute-start | bytes 589832 | tf_op jit(solution)/shard_map/ppermute | solution.py:661
  194.9 97.7 %collective-permute-start.59 = (bf16[128,384]{1,0:T(8,128)(2,1)S(1)}, bf16[128,384]{1,0:T(8,128)(2,1)S(1)}, u32[]{:S(2)}, u32[]{:S(2)}) collective-permute-start(bf16[128,384]{1,0:T(8,128)(2,1)S(1)} %copy-done.74), channel_id=1, source_target_pairs={{0,2},{2,0},{4,6},{6,4},{8,10},{10,8},{12,14},{14,12},{16,18},{18,... | collective-permute-start | bytes 294920 | tf_op jit(solution)/shard_map/ppermute | solution.py:661
  196.3 68.1 %collective-permute-start.72 = (bf16[192,3456]{1,0:T(8,128)(2,1)S(1)}, bf16[192,3456]{1,0:T(8,128)(2,1)S(1)}, u32[]{:S(2)}, u32[]{:S(2)}) collective-permute-start(bf16[192,3456]{1,0:T(8,128)(2,1)S(1)} %get-tuple-element.221), channel_id=1, source_target_pairs={{0,4},{2,6},{4,0},{6,2},{8,12},{10,14},{12,8},{14,10},{16,20},{18,... | collective-permute-start | bytes 3981320 | tf_op jit(solution)/shard_map/ppermute | solution.py:661
  198.9 37.8 %collective-permute-start.22 = (bf16[1,2,256,384]{3,2,1,0:T(8,128)(2,1)S(1)}, bf16[1,2,256,384]{3,2,1,0:T(8,128)(2,1)S(1)}, u32[]{:S(2)}, u32[]{:S(2)}) collective-permute-start(bf16[1,2,256,384]{3,2,1,0:T(8,128)(2,1)S(1)} %fusion.17), channel_id=1, source_target_pairs={{0,4},{2,6},{4,0},{6,2},{8,12},{10,14},{12,8},{14,10},{16,20},{18,... | collective-permute-start | bytes 1179656 | tf_op jit(solution)/shard_map/ppermute | solution.py:661
  200.6 44.5 %collective-permute-start.25 = (bf16[1,2,256,384]{3,2,1,0:T(8,128)(2,1)S(1)}, bf16[1,2,256,384]{3,2,1,0:T(8,128)(2,1)S(1)}, u32[]{:S(2)}, u32[]{:S(2)}) collective-permute-start(bf16[1,2,256,384]{3,2,1,0:T(8,128)(2,1)S(1)} %fusion.19), channel_id=1, source_target_pairs={{0,4},{2,6},{4,0},{6,2},{8,12},{10,14},{12,8},{14,10},{16,20},{18,... | collective-permute-start | bytes 1179656 | tf_op jit(solution)/shard_map/ppermute | solution.py:661
  261.4 28.1 %collective-permute-start.26 = (bf16[1,2,256,384]{3,2,1,0:T(8,128)(2,1)S(1)}, bf16[1,2,256,384]{3,2,1,0:T(8,128)(2,1)S(1)}, u32[]{:S(2)}, u32[]{:S(2)}) collective-permute-start(bf16[1,2,256,384]{3,2,1,0:T(8,128)(2,1)S(1)} %fusion.2), channel_id=1, source_target_pairs={{0,16},{2,18},{4,20},{6,22},{8,24},{10,26},{12,28},{14,30},{16,0},... | collective-permute-start | bytes 1179656 | tf_op jit(solution)/shard_map/ppermute | solution.py:661
  264.4 25.7 %collective-permute-start.29 = (bf16[1,2,256,384]{3,2,1,0:T(8,128)(2,1)S(1)}, bf16[1,2,256,384]{3,2,1,0:T(8,128)(2,1)S(1)}, u32[]{:S(2)}, u32[]{:S(2)}) collective-permute-start(bf16[1,2,256,384]{3,2,1,0:T(8,128)(2,1)S(1)} %fusion.1), channel_id=1, source_target_pairs={{0,8},{2,10},{4,12},{6,14},{8,0},{10,2},{12,4},{14,6},{16,24},{18,... | collective-permute-start | bytes 1179656 | tf_op jit(solution)/shard_map/ppermute | solution.py:661
  267.6 41.8 %collective-permute-start.60 = (bf16[256,768]{1,0:T(8,128)(2,1)S(1)}, bf16[256,768]{1,0:T(8,128)(2,1)S(1)}, u32[]{:S(2)}, u32[]{:S(2)}) collective-permute-start(bf16[256,768]{1,0:T(8,128)(2,1)S(1)} %copy-done.47), channel_id=1, source_target_pairs={{0,2},{2,0},{4,6},{6,4},{8,10},{10,8},{12,14},{14,12},{16,18},{18,... | collective-permute-start | bytes 1179656 | tf_op jit(solution)/shard_map/ppermute | solution.py:661
  297.4 25.5 %collective-permute-start.74 = (bf16[1,48,3456]{2,1,0:T(8,128)(2,1)S(1)}, bf16[1,48,3456]{2,1,0:T(8,128)(2,1)S(1)}, u32[]{:S(2)}, u32[]{:S(2)}) collective-permute-start(bf16[1,48,3456]{2,1,0:T(8,128)(2,1)S(1)} %get-tuple-element.240), channel_id=1, source_target_pairs={{0,16},{2,18},{4,20},{6,22},{8,24},{10,26},{12,28},{14,30},{16,0},... | collective-permute-start | bytes 995336 | tf_op jit(solution)/shard_map/ppermute | solution.py:661
  303.6 19.3 %collective-permute-start.73 = (bf16[1,48,3456]{2,1,0:T(8,128)(2,1)S(1)}, bf16[1,48,3456]{2,1,0:T(8,128)(2,1)S(1)}, u32[]{:S(2)}, u32[]{:S(2)}) collective-permute-start(bf16[1,48,3456]{2,1,0:T(8,128)(2,1)S(1)} %get-tuple-element.238), channel_id=1, source_target_pairs={{0,8},{2,10},{4,12},{6,14},{8,0},{10,2},{12,4},{14,6},{16,24},{18,... | collective-permute-start | bytes 995336 | tf_op jit(solution)/shard_map/ppermute | solution.py:661
  324.7 21.6 %collective-permute-start.47 = (bf16[256,1536]{1,0:T(8,128)(2,1)S(1)}, bf16[256,1536]{1,0:T(8,128)(2,1)}, u32[]{:S(2)}, u32[]{:S(2)}) collective-permute-start(bf16[256,1536]{1,0:T(8,128)(2,1)S(1)} %copy-done.15), channel_id=1, source_target_pairs={{0,2},{2,0},{4,6},{6,4},{8,10},{10,8},{12,14},{14,12},{16,18},{18,... | collective-permute-start | bytes 2359304 | tf_op jit(solution)/shard_map/ppermute | solution.py:661
  325.0 21.2 %collective-permute-start.48 = (bf16[256,768]{1,0:T(8,128)(2,1)}, bf16[256,768]{1,0:T(8,128)(2,1)}, u32[]{:S(2)}, u32[]{:S(2)}) collective-permute-start(bf16[256,768]{1,0:T(8,128)(2,1)} %get-tuple-element.201.refs_4_), channel_id=1, source_target_pairs={{0,2},{2,0},{4,6},{6,4},{8,10},{10,8},{12,14},{14,12},{16,18},{18,... | collective-permute-start | bytes 1179656 | tf_op jit(solution)/shard_map/ppermute | solution.py:661
  325.3 22.1 %collective-permute-start.49 = (bf16[256,1536]{1,0:T(8,128)(2,1)}, bf16[256,1536]{1,0:T(8,128)(2,1)}, u32[]{:S(2)}, u32[]{:S(2)}) collective-permute-start(bf16[256,1536]{1,0:T(8,128)(2,1)} %get-tuple-element.202.refs_6_), channel_id=1, source_target_pairs={{0,2},{2,0},{4,6},{6,4},{8,10},{10,8},{12,14},{14,12},{16,18},{18,... | collective-permute-start | bytes 2359304 | tf_op jit(solution)/shard_map/ppermute | solution.py:661
  329.1 25.3 %collective-permute-start.62 = (bf16[192,2688]{1,0:T(8,128)(2,1)}, bf16[192,2688]{1,0:T(8,128)(2,1)}, u32[]{:S(2)}, u32[]{:S(2)}) collective-permute-start(bf16[192,2688]{1,0:T(8,128)(2,1)} %get-tuple-element.213), channel_id=1, source_target_pairs={{0,4},{2,6},{4,0},{6,2},{8,12},{10,14},{12,8},{14,10},{16,20},{18,... | collective-permute-start | bytes 3096584 | tf_op jit(solution)/shard_map/ppermute | solution.py:661
  357.9 21.8 %collective-permute-start.64 = (bf16[1,48,2688]{2,1,0:T(8,128)(2,1)S(1)}, bf16[1,48,2688]{2,1,0:T(8,128)(2,1)S(1)}, u32[]{:S(2)}, u32[]{:S(2)}) collective-permute-start(bf16[1,48,2688]{2,1,0:T(8,128)(2,1)S(1)} %get-tuple-element.248), channel_id=1, source_target_pairs={{0,16},{2,18},{4,20},{6,22},{8,24},{10,26},{12,28},{14,30},{16,0},... | collective-permute-start | bytes 774152 | tf_op jit(solution)/shard_map/ppermute | solution.py:661
  358.1 21.6 %collective-permute-start.63 = (bf16[1,48,2688]{2,1,0:T(8,128)(2,1)S(1)}, bf16[1,48,2688]{2,1,0:T(8,128)(2,1)S(1)}, u32[]{:S(2)}, u32[]{:S(2)}) collective-permute-start(bf16[1,48,2688]{2,1,0:T(8,128)(2,1)S(1)} %get-tuple-element.246), channel_id=1, source_target_pairs={{0,8},{2,10},{4,12},{6,14},{8,0},{10,2},{12,4},{14,6},{16,24},{18,... | collective-permute-start | bytes 774152 | tf_op jit(solution)/shard_map/ppermute | solution.py:661
  361.6 56.7 %collective-permute-start.50 = (bf16[192,3072]{1,0:T(8,128)(2,1)S(1)}, bf16[192,3072]{1,0:T(8,128)(2,1)S(1)}, u32[]{:S(2)}, u32[]{:S(2)}) collective-permute-start(bf16[192,3072]{1,0:T(8,128)(2,1)S(1)} %copy-done.97), channel_id=1, source_target_pairs={{0,4},{2,6},{4,0},{6,2},{8,12},{10,14},{12,8},{14,10},{16,20},{18,... | collective-permute-start | bytes 3538952 | tf_op jit(solution)/shard_map/ppermute | solution.py:661
  365.4 37.4 %collective-permute-start.42 = (bf16[192,1664]{1,0:T(8,128)(2,1)S(1)}, bf16[192,1664]{1,0:T(8,128)(2,1)S(1)}, u32[]{:S(2)}, u32[]{:S(2)}) collective-permute-start(bf16[192,1664]{1,0:T(8,128)(2,1)S(1)} %get-tuple-element.198), channel_id=1, source_target_pairs={{0,4},{2,6},{4,0},{6,2},{8,12},{10,14},{12,8},{14,10},{16,20},{18,... | collective-permute-start | bytes 1916936 | tf_op jit(solution)/shard_map/ppermute | solution.py:661
  420.6 23.0 %collective-permute-start.52 = (bf16[1,48,3072]{2,1,0:T(8,128)(2,1)S(1)}, bf16[1,48,3072]{2,1,0:T(8,128)(2,1)S(1)}, u32[]{:S(2)}, u32[]{:S(2)}) collective-permute-start(bf16[1,48,3072]{2,1,0:T(8,128)(2,1)S(1)} %get-tuple-element.245), channel_id=1, source_target_pairs={{0,16},{2,18},{4,20},{6,22},{8,24},{10,26},{12,28},{14,30},{16,0},... | collective-permute-start | bytes 884744 | tf_op jit(solution)/shard_map/ppermute | solution.py:661
  420.6 23.0 %collective-permute-start.51 = (bf16[1,48,3072]{2,1,0:T(8,128)(2,1)S(1)}, bf16[1,48,3072]{2,1,0:T(8,128)(2,1)S(1)}, u32[]{:S(2)}, u32[]{:S(2)}) collective-permute-start(bf16[1,48,3072]{2,1,0:T(8,128)(2,1)S(1)} %get-tuple-element.243), channel_id=1, source_target_pairs={{0,8},{2,10},{4,12},{6,14},{8,0},{10,2},{12,4},{14,6},{16,24},{18,... | collective-permute-start | bytes 884744 | tf_op jit(solution)/shard_map/ppermute | solution.py:661
  (146 other events, 1570.0 us)

commit v2 on v1

--- a/solution.py
+++ b/solution.py
@@ -225,34 +225,33 @@
     )
 
 
-def picks_body(pick_ref, band_ref, out_ref):
-    g = pl.program_id(0)
+def picks_body(core_ref, pick_ref, other_ref, band_ref, band_other, out_ref):
+    g = 2 * pl.program_id(0) + core_ref[0]
     heads, picked, R = pick_ref.shape
     half = out_ref.shape[2]
     for h in range(heads):
-        rel = g - band_ref[h : h + 1, :]
-        got = jnp.full((half, R), -1.0, F32)
-        for b in range(picked // half):
-            got = jnp.where(rel == b, pick_ref[h, b * half : (b + 1) * half, :], got)
-        out_ref[0, h // 2, :, (h % 2) * R : (h % 2 + 1) * R] = got
-
-
-def picks(retrieved, band_start, groups, half):
-    R, heads, picked = retrieved.shape
-    pick = (retrieved & 1).astype(F32).transpose(1, 2, 0)
-    band = band_start.T
+        for i, (from_ref, start_ref) in enumerate(((pick_ref, band_ref), (other_ref, band_other))):
+            rel = g - start_ref[h : h + 1, :]
+            got = jnp.full((half, R), -1.0, F32)
+            for b in range(picked // half):
+                got = jnp.where(rel == b, from_ref[h, b * half : (b + 1) * half, :].astype(F32), got)
+            at = (2 * (h % 2) + i) * R
+            out_ref[0, h // 2, :, at : at + R] = got
+
+
+def picks(core_index, pick, pick_other, band, band_other, groups, half):
+    heads, picked, R = pick.shape
     return pl.pallas_call(
         picks_body,
         name="picks",
         grid=(groups,),
-        out_shape=jax.ShapeDtypeStruct((groups, heads // 2, half, 2 * R), F32),
-        in_specs=[
-            pl.BlockSpec((heads, picked, R), lambda g: (0, 0, 0)),
-            pl.BlockSpec((heads, R), lambda g: (0, 0)),
-        ],
-        out_specs=pl.BlockSpec((1, heads // 2, half, 2 * R), lambda g: (g, 0, 0, 0)),
+        out_shape=jax.ShapeDtypeStruct((groups, heads // 2, half, 4 * R), F32),
+        in_specs=[pl.BlockSpec(memory_space=pltpu.SMEM)]
+        + [pl.BlockSpec((heads, picked, R), lambda g: (0, 0, 0))] * 2
+        + [pl.BlockSpec((heads, R), lambda g: (0, 0))] * 2,
+        out_specs=pl.BlockSpec((1, heads // 2, half, 4 * R), lambda g: (g, 0, 0, 0)),
         compiler_params=pltpu.CompilerParams(vmem_limit_bytes=VMEM_LIMIT),
-    )(pick, band)
+    )(core_index, pick, pick_other, band, band_other)
 
 
 def chosen_scores(k2, qq, a):
@@ -269,12 +268,31 @@
     return jnp.concatenate([even, odd], 0)
 
 
-def cross_fwd_body(first, gid_ref, q_ref, *refs):
-    kv, a_refs, refs = refs[:4], refs[4:8], refs[8:]
-    if first:
-        m_ref, l_ref, acc_ref = refs
-    else:
-        m_in, l_in, acc_in, m_ref, l_ref, acc_ref = refs
+def of_both(own, other):
+    return stacked(jnp.concatenate([own, other], 0))
+
+
+def own_lanes(t):
+    R = t.shape[1] // 4
+    return jnp.concatenate([t[:, :R], t[:, 2 * R : 3 * R]], 1)
+
+
+def other_lanes(t):
+    R = t.shape[1] // 4
+    return jnp.concatenate([t[:, R : 2 * R], t[:, 3 * R :]], 1)
+
+
+def all_lanes(own, other):
+    R = own.shape[1] // 2
+    return jnp.concatenate([own[:, :R], other[:, :R], own[:, R:], other[:, R:]], 1)
+
+
+def cross_fwd_body(first, last, gid_ref, q_ref, q_other, *refs):
+    kv, a_refs, refs = refs[:2], refs[2:4], refs[4:]
+    if not first:
+        m_in, l_in, acc_in = refs[:3]
+        refs = refs[3:]
+    m_ref, l_ref, acc_ref = refs[:3]
 
     @pl.when(pl.program_id(0) == 0)
     def _():
@@ -287,16 +305,17 @@
             l_ref[...] = l_in[...]
             acc_ref[...] = acc_in[...]
 
-    for hp in range(acc_ref.shape[0]):
+    pairs = acc_ref.shape[0]
+    for hp in range(pairs):
         sl = slice(hp * PAIR, (hp + 1) * PAIR)
-        qq = stacked(q_ref[:, sl])
-        scores = [chosen_scores(kv[j][0, 0, :, sl], qq, a_refs[j][0, hp]) for j in range(4)]
+        qq = of_both(q_ref[:, sl], q_other[:, sl])
+        scores = [chosen_scores(kv[j][0, 0, :, sl], qq, a_refs[j][0, hp]) for j in range(2)]
         old = m_ref[hp : hp + 1, :]
         top = functools.reduce(jnp.maximum, [jnp.max(s, 0, keepdims=True) for s in scores], old)
         fade = jnp.exp(old - top)
         total = l_ref[hp : hp + 1, :] * fade
         acc = acc_ref[hp] * fade
-        for j in range(4):
+        for j in range(2):
             a = a_refs[j][0, hp]
             p = jnp.where(a < -0.5, 0.0, jnp.exp(scores[j] - top))
             total = total + jnp.sum(p, 0, keepdims=True)
@@ -305,13 +324,25 @@
         l_ref[hp : hp + 1, :] = total
         acc_ref[hp] = acc
 
+    if last:
+        own_ref, other_ref = refs[3:]
+
+        @pl.when(pl.program_id(0) == pl.num_programs(0) - 1)
+        def _():
+            for out, lanes in ((own_ref, own_lanes), (other_ref, other_lanes)):
+                out[pairs * PAIR :, :] = jnp.zeros((8, out.shape[1]), F32)
+                for hp in range(pairs):
+                    out[hp * PAIR : (hp + 1) * PAIR, :] = lanes(acc_ref[hp])
+                    out[pairs * PAIR + hp : pairs * PAIR + hp + 1, :] = lanes(m_ref[hp : hp + 1, :])
+                    out[pairs * PAIR + 4 + hp : pairs * PAIR + 5 + hp, :] = lanes(l_ref[hp : hp + 1, :])
+
 
 def kv_specs(kv, a):
     rows, C = kv[0].shape[2:]
-    specs = [pl.BlockSpec((1, 2, rows, C), lambda i, gid: (i, 0, 0, 0)) for _ in range(4)]
-    for j in range(4):
+    specs = [pl.BlockSpec((1, 2, rows, C), lambda i, gid: (i, 0, 0, 0)) for _ in range(2)]
+    for j in range(2):
         specs.append(
-            pl.BlockSpec((1,) + a.shape[1:], functools.partial(lambda j, i, gid: (gid[4 * i + j], 0, 0, 0), j))
+            pl.BlockSpec((1,) + a.shape[1:], functools.partial(lambda j, i, gid: (gid[2 * i + j], 0, 0, 0), j))
         )
     return specs
 
@@ -320,53 +351,58 @@
     return pl.BlockSpec(shape, lambda i, gid: (0,) * len(shape))
 
 
-def cross_fwd(gid, q, kv, a, state):
-    R, C = q.shape
+def cross_fwd(gid, q, kv, a, state, last):
+    R, C = q[0].shape
     pairs = C // PAIR
-    hi = kv[0].shape[0]
-    rows = kv[0].shape[2]
-    shapes = [(8, 2 * R), (8, 2 * R), (pairs, PAIR, 2 * R)]
+    hi, _, rows, _ = kv[0].shape
+    shapes = [(8, 4 * R), (8, 4 * R), (pairs, PAIR, 4 * R)]
     first = state is None
     state = () if first else tuple(state)
+    if last:
+        shapes += [(C + 8, 2 * R)] * 2
     return pl.pallas_call(
-        functools.partial(cross_fwd_body, first),
+        functools.partial(cross_fwd_body, first, last),
         name="cross_fwd",
         grid_spec=pltpu.PrefetchScalarGridSpec(
             num_scalar_prefetch=1,
             grid=(hi,),
-            in_specs=[fixed(q.shape)] + kv_specs(kv, a) + [fixed(s.shape) for s in state],
+            in_specs=[fixed(q[0].shape)] * 2 + kv_specs(kv, a) + [fixed(s.shape) for s in state],
             out_specs=[fixed(s) for s in shapes],
         ),
         out_shape=[jax.ShapeDtypeStruct(s, F32) for s in shapes],
         compiler_params=pltpu.CompilerParams(vmem_limit_bytes=VMEM_LIMIT),
         cost_estimate=pl.CostEstimate(
-            flops=hi * 4 * 8 * R * rows * C, bytes_accessed=hi * 4 * 4 * rows * C, transcendentals=0
+            flops=hi * 2 * 16 * R * rows * C, bytes_accessed=hi * 2 * 4 * rows * C, transcendentals=0
         ),
-    )(gid, q, *kv, *([a] * 4), *state)
-
-
-def cross_mix_body(m_ref, l_ref, acc_ref, wm, log_ref, of_ref, o_ref, part_ref):
-    pairs = acc_ref.shape[0]
+    )(gid, *q, *kv, *([a] * 2), *state)
+
+
+def cross_mix_body(own_ref, got_ref, wm, log_ref, of_ref, o_ref, part_ref):
+    C = wm.shape[0]
+    pairs = C // PAIR
     log_ref[...] = jnp.zeros(log_ref.shape, F32)
     for hp in range(pairs):
         sl = slice(hp * PAIR, (hp + 1) * PAIR)
-        total = l_ref[hp : hp + 1, :]
-        log_ref[hp : hp + 1, :] = m_ref[hp : hp + 1, :] + jnp.log(total)
-        o = unstacked(acc_ref[hp] * (1.0 / total))
+        m1, m2 = own_ref[C + hp : C + hp + 1, :], got_ref[C + hp : C + hp + 1, :]
+        top = jnp.maximum(m1, m2)
+        f1, f2 = jnp.exp(m1 - top), jnp.exp(m2 - top)
+        total = own_ref[C + 4 + hp : C + 5 + hp, :] * f1 + got_ref[C + 4 + hp : C + 5 + hp, :] * f2
+        log_ref[hp : hp + 1, :] = top + jnp.log(total)
+        o = unstacked((own_ref[sl, :] * f1 + got_ref[sl, :] * f2) * (1.0 / total))
         of_ref[:, sl] = o
         o_ref[:, sl] = o.astype(BF)
     part_ref[...] = nn(o_ref[...], wm[...]).astype(BF)
 
 
-def cross_mix_fwd(m, l, acc, wm):
-    R2 = m.shape[1]
+def cross_mix_fwd(own, got, wm):
+    R2 = own.shape[1]
     C, D = wm.shape
     R = R2 // 2
     return whole(
         cross_mix_body,
         "cross_mix",
         [((8, R2), F32), ((R, C), F32), ((R, C), BF), ((R, D), BF)],
-        m, l, acc, wm,
+        own, got, wm,
         flops=2 * R * C * D,
     )
 
@@ -449,53 +485,58 @@
         gg_ref[1:2, :] += db
 
 
-def cross_mix_back_body(g, dres, own, oth, v_ref, par, of_ref, wm, dv_ref, dlow_ref, do_ref, delta_ref, gg_ref):
+def cross_mix_back_body(g, dres, own, oth, v_ref, par, wm, dv_ref, dlow_ref, do_ref, gg_ref):
     branch_back(g, dres, own, oth, v_ref, par, dv_ref, dlow_ref, gg_ref)
     do_ref[...] = nt(dlow_ref[...], wm[...]).astype(BF)
-    delta_ref[...] = jnp.zeros(delta_ref.shape, F32)
-    for hp in range(do_ref.shape[1] // PAIR):
-        sl = slice(hp * PAIR, (hp + 1) * PAIR)
-        prod = (do_ref[:, sl].astype(F32) * of_ref[:, sl]).T
-        delta_ref[hp : hp + 1, :] = jnp.concatenate(
-            [jnp.sum(prod[:HD], 0, keepdims=True), jnp.sum(prod[HD:], 0, keepdims=True)], 1
-        )
-
-
-def cross_mix_back(g, dres, own, oth, v, par, of, wm):
+
+
+def cross_mix_back(g, dres, own, oth, v, par, wm):
     R, D = v.shape
     C = wm.shape[0]
     return whole(
         functools.partial(cross_mix_back_body, g),
         "cross_mix_back",
-        [((R, D), F32), ((R, D), BF), ((R, C), BF), ((8, 2 * R), F32), ((8, D), F32)],
-        dres, own, oth, v, par, of, wm,
+        [((R, D), F32), ((R, D), BF), ((R, C), BF), ((8, D), F32)],
+        dres, own, oth, v, par, wm,
         flops=2 * R * D * C,
     )
 
 
-def cross_back_body(first, gid_ref, q_ref, do_ref, log_ref, delta_ref, *refs):
-    kv, a_refs, refs = refs[:4], refs[4:8], refs[8:]
+def cross_back_body(first, last, gid_ref, q_ref, q_other, do_ref, do_other, *refs):
+    kv, a_refs, refs = refs[:2], refs[2:4], refs[4:]
     if first:
-        dq_ref, keep_ref, send_ref = refs
+        of_ref, of_other, log_own, log_other = refs[:4]
+        dq_ref, stat_ref, keep_ref, send_ref = refs[4:8]
     else:
-        dq_in, dq_ref, keep_ref, send_ref = refs
+        dq_in, stat_in = refs[:2]
+        dq_ref, stat_ref, keep_ref, send_ref = refs[2:6]
+    pairs = dq_ref.shape[0]
 
     @pl.when(pl.program_id(0) == 0)
     def _():
-        if first:
-            dq_ref[...] = jnp.zeros(dq_ref.shape, F32)
-        else:
+        if not first:
             dq_ref[...] = dq_in[...]
-
-    outs = ((keep_ref, 0), (keep_ref, 1), (send_ref, 0), (send_ref, 1))
-    for hp in range(dq_ref.shape[0]):
+            stat_ref[...] = stat_in[...]
+            return
+        dq_ref[...] = jnp.zeros(dq_ref.shape, F32)
+        stat_ref[...] = jnp.zeros(stat_ref.shape, F32)
+        stat_ref[0:8, :] = all_lanes(log_own[...], log_other[...])
+        for hp in range(pairs):
+            sl = slice(hp * PAIR, (hp + 1) * PAIR)
+            sums = []
+            for d, o in ((do_ref, of_ref), (do_other, of_other)):
+                prod = (d[:, sl].astype(F32) * o[:, sl]).T
+                sums.append([jnp.sum(prod[:HD], 0, keepdims=True), jnp.sum(prod[HD:], 0, keepdims=True)])
+            stat_ref[8 + hp : 9 + hp, :] = jnp.concatenate([sums[0][0], sums[1][0], sums[0][1], sums[1][1]], 1)
+
+    for hp in range(pairs):
         sl = slice(hp * PAIR, (hp + 1) * PAIR)
-        qq = stacked(q_ref[:, sl])
-        dd = stacked(do_ref[:, sl])
-        log_total = log_ref[hp : hp + 1, :]
-        delta = delta_ref[hp : hp + 1, :]
+        qq = of_both(q_ref[:, sl], q_other[:, sl])
+        dd = of_both(do_ref[:, sl], do_other[:, sl])
+        log_total = stat_ref[hp : hp + 1, :]
+        delta = stat_ref[8 + hp : 9 + hp, :]
         dq = dq_ref[hp]
-        for j in range(4):
+        for j, out_ref in enumerate((keep_ref, send_ref)):
             a = a_refs[j][0, hp]
             half = a.shape[0]
             k2 = kv[j][0, 0, :, sl]
@@ -503,53 +544,61 @@
             daT = nt(kv[j][0, 1, :, sl], dd)
             ds = p * (jnp.where(a > 0.5, daT[half:], daT[:half]) - delta)
             dsT = spread(ds, a)
-            out_ref, y = outs[j]
-            out_ref[0, y, 0, :, sl] = nn(dsT, qq).astype(BF)
-            out_ref[0, y, 1, :, sl] = nn(spread(p, a), dd).astype(BF)
+            out_ref[0, 0, :, sl] = nn(dsT, qq).astype(BF)
+            out_ref[0, 1, :, sl] = nn(spread(p, a), dd).astype(BF)
             dq = dq + tn(k2, dsT)
         dq_ref[hp] = dq
 
-
-def cross_back(gid, q, do, log_total, delta, kv, a, dq):
-    R, C = q.shape
+    if last:
+        own_ref, other_ref = refs[-2:]
+
+        @pl.when(pl.program_id(0) == pl.num_programs(0) - 1)
+        def _():
+            for hp in range(pairs):
+                own_ref[hp] = own_lanes(dq_ref[hp])
+                other_ref[hp] = other_lanes(dq_ref[hp])
+
+
+def cross_back(gid, q, do, kv, a, extra, first, last):
+    R, C = q[0].shape
     pairs = C // PAIR
     hi, _, rows, _ = kv[0].shape
-    first = dq is None
-    extra = () if first else (dq,)
-    dq_shape = (pairs, PAIR, 2 * R)
-    grad_spec = pl.BlockSpec((1, 2, 2, rows, C), lambda i, gid: (i, 0, 0, 0, 0))
-    grad_shape = jax.ShapeDtypeStruct((hi, 2, 2, rows, C), BF)
+    grad_spec = pl.BlockSpec((1, 2, rows, C), lambda i, gid: (i, 0, 0, 0))
+    shapes = [(pairs, PAIR, 4 * R), (16, 4 * R)]
+    out_specs = [fixed(s) for s in shapes] + [grad_spec] * 2
+    out_shape = [jax.ShapeDtypeStruct(s, F32) for s in shapes] + [jax.ShapeDtypeStruct(kv[0].shape, BF)] * 2
+    if last:
+        out_specs += [fixed((pairs, PAIR, 2 * R))] * 2
+        out_shape += [jax.ShapeDtypeStruct((pairs, PAIR, 2 * R), F32)] * 2
     return pl.pallas_call(
-        functools.partial(cross_back_body, first),
+        functools.partial(cross_back_body, first, last),
         name="cross_back",
         grid_spec=pltpu.PrefetchScalarGridSpec(
             num_scalar_prefetch=1,
             grid=(hi,),
-            in_specs=[fixed(q.shape), fixed(do.shape), fixed(log_total.shape), fixed(delta.shape)]
-            + kv_specs(kv, a)
-            + [fixed(e.shape) for e in extra],
-            out_specs=[fixed(dq_shape), grad_spec, grad_spec],
+            in_specs=[fixed(q[0].shape)] * 4 + kv_specs(kv, a) + [fixed(e.shape) for e in extra],
+            out_specs=out_specs,
         ),
-        out_shape=[jax.ShapeDtypeStruct(dq_shape, F32), grad_shape, grad_shape],
+        out_shape=out_shape,
         compiler_params=pltpu.CompilerParams(vmem_limit_bytes=VMEM_LIMIT),
         cost_estimate=pl.CostEstimate(
-            flops=hi * 4 * 20 * R * rows * C, bytes_accessed=hi * 4 * 8 * rows * C, transcendentals=0
+            flops=hi * 2 * 40 * R * rows * C, bytes_accessed=hi * 2 * 8 * rows * C, transcendentals=0
         ),
-    )(gid, q, do, log_total, delta, *kv, *([a] * 4), *extra)
-
-
-def cross_q_back_body(dq_in, wq, dq_ref, part_ref):
-    for hp in range(dq_in.shape[0]):
+    )(gid, *q, *do, *kv, *([a] * 2), *extra)
+
+
+def cross_q_back_body(dq_own, dq_got, wq, dq_ref, part_ref):
+    for hp in range(dq_own.shape[0]):
         sl = slice(hp * PAIR, (hp + 1) * PAIR)
-        dq_ref[:, sl] = (unstacked(dq_in[hp]) * SCALE).astype(BF)
+        dq_ref[:, sl] = (unstacked(dq_own[hp] + dq_got[hp]) * SCALE).astype(BF)
     part_ref[...] = nt(dq_ref[...], wq[...]).astype(BF)
 
 
-def cross_q_back(dq, wq):
+def cross_q_back(dq, got, wq):
     D, C = wq.shape
     R = dq.shape[2] // 2
     return whole(
-        cross_q_back_body, "cross_q_back", [((R, C), BF), ((R, D), BF)], dq, wq, flops=2 * R * D * C
+        cross_q_back_body, "cross_q_back", [((R, C), BF), ((R, D), BF)], dq, got, wq, flops=2 * R * D * C
     )
 
 
@@ -668,10 +717,9 @@
 def scatter_sum(keep, send, n):
     total = keep.astype(F32) + swap(send, 2, n).astype(F32)
     total = total.reshape(4, n // 16, -1, total.shape[1])
-    low = total.astype(BF)
-    total = total[0]
-    for k in range(1, 4):
-        total = total + swap(low[k], 4 * k, n).astype(F32)
+    far = swap(jnp.stack([total[1], total[3]]).astype(BF), 4, n).astype(F32)
+    total, away = total[0] + far[0], total[2] + far[1]
+    total = total + swap(away.astype(BF), 8, n).astype(F32)
     bit = n // 2
     while total.shape[0] > 1:
         half = total.shape[0] // 2
@@ -737,7 +785,9 @@
     enc_other = other_tp(enc_part)
     *self_kept, self_o, self_part = attend_fwd(decoder_in, self_query, self_key, self_value, self_mix, lengths)
     self_other = other_tp(self_part)
-    chosen = picks(retrieved, band_start, n, group_rows // 2)
+    pick = (retrieved & 1).astype(BF).transpose(1, 2, 0)
+    band = band_start.T
+    chosen = picks((me & 1).reshape(1), pick, core(pick), band, core(band), n // 2, group_rows // 2)
 
     v1, u1, low1, act1, gp1, part1 = ffn_fwd(0, encoder_in, enc_part, enc_other, par, enc_up, enc_down)
     other1 = other_tp(part1)
@@ -747,18 +797,17 @@
     store = store[None]
     for b in range(4, n.bit_length() - 1):
         store = jnp.concatenate([store, swap(store, 1 << b, n)], 0)
-    pieces = []
-    gids = []
-    for k in range(4):
-        z = store if k == 0 else swap(store, 4 * k, n)
-        y = swap(z, 2, n)
-        pieces.append((z, y, core(z), core(y)))
-        rel = [16 * h + 4 * k + r for h in range(hi) for r in (0, 2, 1, 3)]
-        gids.append(me ^ jnp.array(rel, jnp.int32))
+    near = swap(store, 4, n)
+    far = swap(store, 8, n)
+    apart = swap(far, 4, n)
+    pieces = [(z, swap(z, 2, n)) for z in (store, near, far, apart)]
+    rels = [[16 * h + 4 * k + r for h in range(hi) for r in (0, 2)] for k in range(4)]
+    gids = [(me ^ jnp.array(rel, jnp.int32)) >> 1 for rel in rels]
+    qcs = (qc, core(qc))
     state = None
     for k in range(4):
-        state = cross_fwd(gids[k], qc, pieces[k], chosen, state)
-    log_total, of, oc, partc = cross_mix_fwd(*state, cross_mix)
+        state = cross_fwd(gids[k], qcs, pieces[k], chosen, state, k == 3)
+    log_total, of, oc, partc = cross_mix_fwd(state[3], core(state[4]), cross_mix)
     otherc = other_tp(partc)
     vc, uc, lowc, actc, gpc, part3 = ffn_fwd(6, ud, partc, otherc, par, dec_up, dec_down)
     other3 = other_tp(part3)
@@ -766,7 +815,7 @@
         8, uc, part3, other3, cotangent, par, gpc, dec_up, dec_down
     )
     other4 = other_tp(part4)
-    dcross, dcross_low, do, delta, gg_cross = cross_mix_back(6, dlast, part4, other4, vc, par, of, cross_mix)
+    dcross, dcross_low, do, gg_cross = cross_mix_back(6, dlast, part4, other4, vc, par, cross_mix)
 
     both = lambda x: (x, core(x))
     first_sum = scatter_sum(
@@ -781,22 +830,25 @@
         n,
     )
 
-    dq = None
-    terms = []
+    dos = (do, core(do))
+    extra = (of, core(of), log_total, core(log_total))
+    kept = {}
     for k in (3, 2, 1, 0):
-        dq, keep, send = cross_back(gids[k], qc, do, log_total, delta, pieces[k], chosen, dq)
-        got = core(send)
-        mine = (keep[:, 0].astype(F32) + got[:, 0].astype(F32)).astype(BF)
-        away = (keep[:, 1].astype(F32) + got[:, 1].astype(F32)).astype(BF)
-        mine = (mine.astype(F32) + swap(away, 2, n).astype(F32)).astype(BF)
-        terms.append(mine if k == 0 else swap(mine, 4 * k, n))
+        dq, stat, keep, send, *dq_halves = cross_back(gids[k], qcs, dos, pieces[k], chosen, extra, k == 3, k == 0)
+        extra = (dq, stat)
+        kept[k] = (keep, swap(send, 2, n))
+    summed = lambda *arrays: functools.reduce(lambda x, y: x + y, [t.astype(F32) for t in arrays]).astype(BF)
+    apart = swap(summed(*kept[3]), 4, n)
+    far = swap(summed(*kept[2], apart), 8, n)
+    near = swap(summed(*kept[1]), 4, n)
+    terms = [*kept[0], near, far]
     bit = n // 2
     while terms[0].shape[0] > 1:
         half = terms[0].shape[0] // 2
         total = functools.reduce(lambda x, y: x + y, [t.astype(F32) for t in terms])
         terms = [total[:half].astype(BF), swap(total[half:].astype(BF), bit, n)]
         bit //= 2
-    dqc, partq = cross_q_back(dq, cross_query)
+    dqc, partq = cross_q_back(dq_halves[0], core(dq_halves[1]), cross_query)
     otherq = other_tp(partq)
     dkv, part5 = store_back(terms, cross_key, cross_value)
     other5 = other_tp(part5)

time: 452 us -> 379 us (0.84)
  waiting for transfers between devices: 229 us -> 171 us
  Pallas kernels: 97 us -> 91.3 us
  starting transfers between devices: 64 us -> 59.4 us
    ppermute x65 -> x57, waiting for transfers between devices: 185 us -> 127 us  [swap(): return lax.ppermute(x, 'blk', [(i, i ^ bit) for i in range(n)])]
    convert_element_type x12 -> x11, other arithmetic: 10.5 us -> 2.69 us  [the longest x4 1.38 us: scatter_sum(): far = swap(jnp.stack([total[1], total[3]]).astype(BF), 4, n).astype(F32)]
    ppermute x65 -> x57, starting transfers between devices: 49.4 us -> 43 us  [swap(): return lax.ppermute(x, 'blk', [(i, i ^ bit) for i in range(n)])]
    add x0 -> x4, other arithmetic: none -> 5.29 us  [scatter_sum(): total = keep.astype(F32) + swap(send, 2, n).astype(F32)]
    pallas_call x8, Pallas kernels: 42.1 us -> 37.2 us  [the longest x4 20.6 us: cross_back(): pl.pallas_call(functools.partial(cross_back_body, first, last), name='cro...]
    unnamed x205 -> x183, local copies, waits for them, and re-layouts: 28.9 us -> 27.1 us
  transfers between devices with their start and end apart: 76 -> 68, of which waited for: 29 -> 24; matrix products, arithmetic and copies ran while one was open for 6% -> 6% of each run, Pallas kernels for 16% -> 21%
where the time goes in v2:
time: 379 us; the launch traced here: 372 us
  waiting for transfers between devices  171 us (45%)
  Pallas kernels  91.3 us (24%)
  starting transfers between devices  59.4 us (16%)
  local copies, waits for them, and re-layouts  32.2 us (8%)
  other arithmetic  14.7 us (4%)
    ppermute x57, waiting for transfers between devices, swap(): return lax.ppermute(x, 'blk', [(i, i ^ bit) for i in range(n)])  127 us
    pallas_call x18, Pallas kernels, whole(): pl.pallas_call(body, name=name, out_shape=[jax.ShapeDtypeStruct(s, d) for...  46.2 us
    ppermute x11, waiting for transfers between devices, other_tp(): return lax.ppermute(x, 'tp', [(0, 1), (1, 0)])  43.9 us
    ppermute x57, starting transfers between devices, swap(): return lax.ppermute(x, 'blk', [(i, i ^ bit) for i in range(n)])  43 us
    unnamed x183, local copies, waits for them, and re-layouts  27.1 us
    pallas_call x4, Pallas kernels, cross_back(): pl.pallas_call(functools.partial(cross_back_body, first, last), name='cro...  20.6 us
    pallas_call x4, Pallas kernels, cross_fwd(): pl.pallas_call(functools.partial(cross_fwd_body, first, last), name='cros...  16.6 us
    ppermute x11, starting transfers between devices, other_tp(): return lax.ppermute(x, 'tp', [(0, 1), (1, 0)])  16.4 us
  transfers between devices with their start and end apart: 68, of which 24 were waited for; matrix products, arithmetic and copies ran while one was open for 6% of the time, Pallas kernels for 21%

profile of v2, /device:TPU:0, one launch (start us, length us, event | category | flops | bytes accessed | tf_op | source)
XLA Modules:
  0.0 371.9 jit_solution(5212999943470183807)
XLA Ops:
  22.9 4.4 %ffn_fwd.2 = (f32[256,768]{1,0:T(8,128)S(1)}, f32[256,768]{1,0:T(8,128)S(1)}, bf16[256,768]{1,0:T(8,128)(2,1)S(1)}, bf16[256,1536]{1,0:T(8,128)(2,1)S(1)}, bf16[...) custom-call(bf16[256,768]{1,0:T(8,128)(2,1)S(1)} %copy-done.17, bf16[256,768]{1,0:T(8,128)(2,1)S(1)} %get-tuple-element.128.own, ...), custom_call_target="tpu_custom_call" | custom-call | flops 1207959552 | bytes 9845760 | tf_op jit(solution)/shard_map/ffn_fwd/pallas_call | solution.py:36
  31.8 8.6 %collective-permute-done.1.oth = bf16[256,768]{1,0:T(8,128)(2,1)S(1)} collective-permute-done((bf16[256,768]{1,0:T(8,128)(2,1)S(1)}, bf16[256,768]{1,0:T(8,128)(2,1)S(1)}, u32[]{:S(2)}, u32[]{:S(2)}) %collective-permute-start.1) | collective-permute-done | bytes 393248 | tf_op jit(solution)/shard_map/ppermute | solution.py:714
  53.2 9.2 %collective-permute-done.4.refs_0_ = bf16[1,2,256,384]{3,2,1,0:T(8,128)(2,1)} collective-permute-done((bf16[1,2,256,384]{3,2,1,0:T(8,128)(2,1)}, bf16[1,2,256,384]{3,2,1,0:T(8,128)(2,1)}, u32[]{:S(2)}, u32[]{:S(2)}) %collective-permute-start.4) | collective-permute-done | bytes 393248 | tf_op jit(solution)/shard_map/ppermute | solution.py:710
  66.3 6.7 %collective-permute-done.5.refs_0_ = bf16[1,2,256,384]{3,2,1,0:T(8,128)(2,1)} collective-permute-done((bf16[1,2,256,384]{3,2,1,0:T(8,128)(2,1)}, bf16[1,2,256,384]{3,2,1,0:T(8,128)(2,1)}, u32[]{:S(2)}, u32[]{:S(2)}) %collective-permute-start.5) | collective-permute-done | bytes 393248 | tf_op jit(solution)/shard_map/ppermute | solution.py:710
  76.3 7.8 %picks.1.refs_2_.refs_3_ = f32[8,3,128,512]{3,2,1,0:T(8,128)} custom-call(s32[1]{0:T(128)} %bitcast.1.core_ref, bf16[6,1024,128]{2,1,0:T(8,128)(2,1)S(1)} %fusion.pick_ref, bf16[6,1024,128]{2,1,0:T(8,128)(2,1)} %collective-permute-done.7.other_ref, s32[6,128]{1,0:T(8,128)S(1)} %bitcast.144, s32[6,128]{1,0:T(8,128)S(1)} %collective-permute-done.8.band_other), custom_call_target="tpu_custom_call" | custom-call | tf_op jit(solution)/shard_map/picks/pallas_call | solution.py:244
  84.2 3.9 %cross_fwd.4 = (f32[8,512]{1,0:T(8,128)S(1)}, f32[8,512]{1,0:T(8,128)S(1)}, f32[3,128,512]{2,1,0:T(8,128)S(1)}) custom-call(s32[2]{0:T(128)S(1)} %xor_shift-right-arithmetic_fusion.gid_ref, bf16[128,384]{1,0:T(8,128)(2,1)S(1)} %get-tuple-element.134.q_ref, bf16[128,384]{1,0:T(8,128)(2,1)S(1)} %collective-permute-done.3.q_other, ...), custom_call_target="tpu_custom_call" | custom-call | flops 402653184 | bytes 786432 | tf_op jit(solution)/shard_map/cross_fwd/pallas_call | solution.py:363
  88.1 3.9 %cross_fwd.5 = (f32[8,512]{1,0:T(8,128)S(1)}, f32[8,512]{1,0:T(8,128)S(1)}, f32[3,128,512]{2,1,0:T(8,128)S(1)}) custom-call(s32[2]{0:T(128)S(1)} %xor_shift-right-arithmetic_fusion.1.gid_ref, bf16[128,384]{1,0:T(8,128)(2,1)S(1)} %get-tuple-element.134.q_ref, bf16[128,384]{1,0:T(8,128)(2,1)S(1)} %collective-permute-done.3.q_other, ...), custom_call_target="tpu_custom_call" | custom-call | flops 402653184 | bytes 786432 | tf_op jit(solution)/shard_map/cross_fwd/pallas_call | solution.py:363
  98.9 5.0 %cross_fwd.7 = (f32[8,512]{1,0:T(8,128)}, f32[8,512]{1,0:T(8,128)}, f32[3,128,512]{2,1,0:T(8,128)}, f32[392,256]{1,0:T(8,128)S(1)}, f32[392,256]{1,0:T(8,128)S(1)}) custom-call(s32[2]{0:T(128)S(1)} %xor_shift-right-arithmetic_fusion.3.gid_ref, bf16[128,384]{1,0:T(8,128)(2,1)S(1)} %get-tuple-element.134.q_ref, ...), custom_call_target="tpu_custom_call" | custom-call | flops 402653184 | bytes 786432 | tf_op jit(solution)/shard_map/cross_fwd/pallas_call | solution.py:363
  107.5 5.5 %collective-permute-done.14.oth = bf16[128,768]{1,0:T(8,128)(2,1)S(1)} collective-permute-done((bf16[128,768]{1,0:T(8,128)(2,1)S(1)}, bf16[128,768]{1,0:T(8,128)(2,1)S(1)}, u32[]{:S(2)}, u32[]{:S(2)}) %collective-permute-start.14) | collective-permute-done | bytes 196640 | tf_op jit(solution)/shard_map/ppermute | solution.py:714
  117.4 4.6 %collective-permute-done.15.oth = bf16[128,768]{1,0:T(8,128)(2,1)S(1)} collective-permute-done((bf16[128,768]{1,0:T(8,128)(2,1)S(1)}, bf16[128,768]{1,0:T(8,128)(2,1)S(1)}, u32[]{:S(2)}, u32[]{:S(2)}) %collective-permute-start.15) | collective-permute-done | bytes 196640 | tf_op jit(solution)/shard_map/ppermute | solution.py:714
  122.1 4.2 %last_fwd_back.1 = (f32[128,768]{1,0:T(8,128)}, f32[128,768]{1,0:T(8,128)S(1)}, bf16[128,768]{1,0:T(8,128)(2,1)S(1)}, bf16[128,1536]{1,0:T(8,128)(2,1)S(1)}, f32...) custom-call(f32[128,768]{1,0:T(8,128)S(1)} %get-tuple-element.148.u_ref, bf16[128,768]{1,0:T(8,128)(2,1)S(1)} %get-tuple-element.149.own, ...), custom_call_target="tpu_custom_call" | custom-call | flops 603979776 | bytes 7707648 | tf_op jit(solution)/shard_map/last_fwd_back/pallas_call | solution.py:36
  127.7 4.2 %collective-permute-done.16.oth = bf16[128,768]{1,0:T(8,128)(2,1)S(1)} collective-permute-done((bf16[128,768]{1,0:T(8,128)(2,1)S(1)}, bf16[128,768]{1,0:T(8,128)(2,1)S(1)}, u32[]{:S(2)}, u32[]{:S(2)}) %collective-permute-start.16) | collective-permute-done | bytes 196640 | tf_op jit(solution)/shard_map/ppermute | solution.py:714
  134.8 5.0 %cross_back.4 = (f32[3,128,512]{2,1,0:T(8,128)S(1)}, f32[16,512]{1,0:T(8,128)S(1)}, bf16[1,2,256,384]{3,2,1,0:T(8,128)(2,1)S(1)}, bf16[1,2,256,384]{3,2,1,0:T(8,128)(2,1)S(1)}) custom-call(s32[2]{0:T(128)S(1)} %xor_shift-right-arithmetic_fusion.3.gid_ref, bf16[128,384]{1,0:T(8,128)(2,1)S(1)} %get-tuple-element.134.q_ref, ...), custom_call_target="tpu_custom_call" | custom-call | flops 1006632960 | bytes 1572864 | tf_op jit(solution)/shard_map/cross_back/pallas_call | solution.py:573
  142.2 4.8 %cross_back.5 = (f32[3,128,512]{2,1,0:T(8,128)S(1)}, f32[16,512]{1,0:T(8,128)S(1)}, bf16[1,2,256,384]{3,2,1,0:T(8,128)(2,1)S(1)}, bf16[1,2,256,384]{3,2,1,0:T(8,128)(2,1)S(1)}) custom-call(s32[2]{0:T(128)S(1)} %xor_shift-right-arithmetic_fusion.2.gid_ref, bf16[128,384]{1,0:T(8,128)(2,1)S(1)} %get-tuple-element.134.q_ref, ...), custom_call_target="tpu_custom_call" | custom-call | flops 1006632960 | bytes 1572864 | tf_op jit(solution)/shard_map/cross_back/pallas_call | solution.py:573
  147.0 4.9 %cross_back.6 = (f32[3,128,512]{2,1,0:T(8,128)S(1)}, f32[16,512]{1,0:T(8,128)S(1)}, bf16[1,2,256,384]{3,2,1,0:T(8,128)(2,1)S(1)}, bf16[1,2,256,384]{3,2,1,0:T(8,128)(2,1)S(1)}) custom-call(s32[2]{0:T(128)S(1)} %xor_shift-right-arithmetic_fusion.1.gid_ref, bf16[128,384]{1,0:T(8,128)(2,1)S(1)} %get-tuple-element.134.q_ref, ...), custom_call_target="tpu_custom_call" | custom-call | flops 1006632960 | bytes 1572864 | tf_op jit(solution)/shard_map/cross_back/pallas_call | solution.py:573
  158.1 5.8 %cross_back.7 = (f32[3,128,512]{2,1,0:T(8,128)}, f32[16,512]{1,0:T(8,128)}, bf16[1,2,256,384]{3,2,1,0:T(8,128)(2,1)S(1)}, bf16[1,2,256,384]{3,2,1,0:T(8,128)(2,1...) custom-call(s32[2]{0:T(128)S(1)} %xor_shift-right-arithmetic_fusion.gid_ref, ...), custom_call_target="tpu_custom_call" | custom-call | flops 1006632960 | bytes 1572864 | tf_op jit(solution)/shard_map/cross_back/pallas_call | solution.py:573
  164.9 7.6 %collective-permute-done.23 = bf16[1,2,256,384]{3,2,1,0:T(8,128)(2,1)S(1)} collective-permute-done((bf16[1,2,256,384]{3,2,1,0:T(8,128)(2,1)S(1)}, bf16[1,2,256,384]{3,2,1,0:T(8,128)(2,1)S(1)}, u32[]{:S(2)}, u32[]{:S(2)}) %collective-permute-start.23) | collective-permute-done | bytes 393248 | tf_op jit(solution)/shard_map/ppermute | solution.py:710
  178.7 4.2 %collective-permute-done.31.refs_3_ = bf16[128,768]{1,0:T(8,128)(2,1)S(1)} collective-permute-done((bf16[128,768]{1,0:T(8,128)(2,1)S(1)}, bf16[128,768]{1,0:T(8,128)(2,1)S(1)}, u32[]{:S(2)}, u32[]{:S(2)}) %collective-permute-start.31) | collective-permute-done | bytes 196640 | tf_op jit(solution)/shard_map/ppermute | solution.py:714
  185.6 22.9 %collective-permute-done.20.refs_1_ = bf16[1,2,256,384]{3,2,1,0:T(8,128)(2,1)S(1)} collective-permute-done((bf16[1,2,256,384]{3,2,1,0:T(8,128)(2,1)S(1)}, bf16[1,2,256,384]{3,2,1,0:T(8,128)(2,1)S(1)}, u32[]{:S(2)}, u32[]{:S(2)}) %collective-permute-start.20) | collective-permute-done | bytes 393248 | tf_op jit(solution)/shard_map/ppermute | solution.py:710
  214.9 6.7 %collective-permute-done.27.oth = bf16[256,768]{1,0:T(8,128)(2,1)S(1)} collective-permute-done((bf16[256,768]{1,0:T(8,128)(2,1)S(1)}, bf16[256,768]{1,0:T(8,128)(2,1)S(1)}, u32[]{:S(2)}, u32[]{:S(2)}) %collective-permute-start.27) | collective-permute-done | bytes 393248 | tf_op jit(solution)/shard_map/ppermute | solution.py:714
  223.1 4.5 %ffn_back.1 = (f32[256,768]{1,0:T(8,128)S(1)}, bf16[256,768]{1,0:T(8,128)(2,1)S(1)}, bf16[256,1536]{1,0:T(8,128)(2,1)S(1)}, f32[8,768]{1,0:T(8,128)S(1)}, bf16[256,768]{1,0:T(8,128)(2,1)S(1)}) custom-call(bf16[256,768]{1,0:T(8,128)(2,1)S(1)} %get-tuple-element.172.own, bf16[256,768]{1,0:T(8,128)(2,1)S(1)} %collective-permute-done.27.oth, ...), custom_call_target="tpu_custom_call" | custom-call | flops 1207959552 | bytes 9477120 | tf_op jit(solution)/shard_map/ffn_back/pallas_call | solution.py:36
  231.2 7.0 %collective-permute-done.28.refs_2_ = bf16[256,768]{1,0:T(8,128)(2,1)S(1)} collective-permute-done((bf16[256,768]{1,0:T(8,128)(2,1)S(1)}, bf16[256,768]{1,0:T(8,128)(2,1)S(1)}, u32[]{:S(2)}, u32[]{:S(2)}) %collective-permute-start.28) | collective-permute-done | bytes 393248 | tf_op jit(solution)/shard_map/ppermute | solution.py:714
  238.3 5.0 %attend_back.2 = (f32[256,768]{1,0:T(8,128)S(1)}, bf16[256,768]{1,0:T(8,128)(2,1)S(1)}, bf16[256,1152]{1,0:T(8,128)(2,1)S(1)}, f32[8,768]{1,0:T(8,128)S(1)}, bf16[256,768]{1,0:T(8,128)(2,1)S(1)}) custom-call(f32[256,768]{1,0:T(8,128)} %copy-done.26, bf16[256,768]{1,0:T(8,128)(2,1)S(1)} %get-tuple-element.176.refs_1_, ...), custom_call_target="tpu_custom_call" | custom-call | flops 1107296256 | bytes 7511040 | tf_op jit(solution)/shard_map/attend_back/pallas_call | solution.py:36
  253.5 4.1 %weight_grads.6 = (bf16[192,2688]{1,0:T(8,128)(2,1)S(1)}, bf16[192,2688]{1,0:T(8,128)(2,1)S(1)}) custom-call(s32[384,1]{1,0:T(8,128)S(1)} %fusion.38.idx_ref, bf16[128,768]{1,0:T(8,128)(2,1)S(1)} %copy-done.60, bf16[128,768]{1,0:T(8,128)(2,1)S(1)} %copy-done.64, bf16[128,384]{1,0:T(8,128)(2,1)} %get-tuple-element.210.refs_2_, ...), custom_call_target="tpu_custom_call" | custom-call | flops 679477248 | bytes 5801472 | tf_op jit(solution)/shard_map/weight_grads/pallas_call | solution.py:36
  265.2 3.9 %weight_grads.5 = (bf16[192,3072]{1,0:T(8,128)(2,1)S(1)}, bf16[192,3072]{1,0:T(8,128)(2,1)}) custom-call(s32[384,1]{1,0:T(8,128)S(1)} %fusion.38.idx_ref, bf16[256,768]{1,0:T(8,128)(2,1)S(1)} %copy-done.42, bf16[256,768]{1,0:T(8,128)(2,1)S(1)} %collective-permute-done.41.refs_1_, bf16[256,1536]{1,0:T(8,128)(2,1)S(1)} %copy-done.20, ...), custom_call_target="tpu_custom_call" | custom-call | flops 1207959552 | bytes 7079424 | tf_op jit(solution)/shard_map/weight_grads/pallas_call | solution.py:36
  270.4 9.8 %collective-permute-done.67 = bf16[1,48,3456]{2,1,0:T(8,128)(2,1)} collective-permute-done((bf16[1,48,3456]{2,1,0:T(8,128)(2,1)}, bf16[1,48,3456]{2,1,0:T(8,128)(2,1)}, u32[]{:S(2)}, u32[]{:S(2)}) %collective-permute-start.67) | collective-permute-done | bytes 331808 | tf_op jit(solution)/shard_map/ppermute | solution.py:710
  281.2 5.0 %collective-permute-done.56 = bf16[192,2688]{1,0:T(8,128)(2,1)} collective-permute-done((bf16[192,2688]{1,0:T(8,128)(2,1)S(1)}, bf16[192,2688]{1,0:T(8,128)(2,1)}, u32[]{:S(2)}, u32[]{:S(2)}) %collective-permute-start.56) | collective-permute-done | bytes 1032224 | tf_op jit(solution)/shard_map/ppermute | solution.py:710
  294.0 6.7 %collective-permute-done.57 = bf16[2,1,48,2688]{3,2,1,0:T(8,128)(2,1)S(1)} collective-permute-done((bf16[2,1,48,2688]{3,2,1,0:T(8,128)(2,1)S(1)}, bf16[2,1,48,2688]{3,2,1,0:T(8,128)(2,1)S(1)}, u32[]{:S(2)}, u32[]{:S(2)}) %collective-permute-start.57) | collective-permute-done | bytes 516128 | tf_op jit(solution)/shard_map/ppermute | solution.py:710
  304.6 25.6 %collective-permute-done.38 = bf16[192,1664]{1,0:T(8,128)(2,1)S(1)} collective-permute-done((bf16[192,1664]{1,0:T(8,128)(2,1)S(1)}, bf16[192,1664]{1,0:T(8,128)(2,1)S(1)}, u32[]{:S(2)}, u32[]{:S(2)}) %collective-permute-start.38) | collective-permute-done | bytes 639008 | tf_op jit(solution)/shard_map/ppermute | solution.py:710
  332.3 5.7 %collective-permute-done.39 = bf16[2,1,48,1664]{3,2,1,0:T(8,128)(2,1)S(1)} collective-permute-done((bf16[2,1,48,1664]{3,2,1,0:T(8,128)(2,1)S(1)}, bf16[2,1,48,1664]{3,2,1,0:T(8,128)(2,1)S(1)}, u32[]{:S(2)}, u32[]{:S(2)}) %collective-permute-start.39) | collective-permute-done | bytes 319520 | tf_op jit(solution)/shard_map/ppermute | solution.py:710
  346.2 10.0 %collective-permute-done.46 = bf16[2,1,48,3072]{3,2,1,0:T(8,128)(2,1)S(1)} collective-permute-done((bf16[2,1,48,3072]{3,2,1,0:T(8,128)(2,1)S(1)}, bf16[2,1,48,3072]{3,2,1,0:T(8,128)(2,1)S(1)}, u32[]{:S(2)}, u32[]{:S(2)}) %collective-permute-start.46) | collective-permute-done | bytes 589856 | tf_op jit(solution)/shard_map/ppermute | solution.py:710
  359.3 11.1 %collective-permute-done.47 = bf16[1,48,3072]{2,1,0:T(8,128)(2,1)S(1)} collective-permute-done((bf16[1,48,3072]{2,1,0:T(8,128)(2,1)S(1)}, bf16[1,48,3072]{2,1,0:T(8,128)(2,1)S(1)}, u32[]{:S(2)}, u32[]{:S(2)}) %collective-permute-start.47) | collective-permute-done | bytes 294944 | tf_op jit(solution)/shard_map/ppermute | solution.py:710
  (376 shorter events, 140.4 us)
Async XLA Ops:
  19.7 56.5 %collective-permute-start.7 = (bf16[6,1024,128]{2,1,0:T(8,128)(2,1)S(1)}, bf16[6,1024,128]{2,1,0:T(8,128)(2,1)}, u32[]{:S(2)}, u32[]{:S(2)}) collective-permute-start(bf16[6,1024,128]{2,1,0:T(8,128)(2,1)S(1)} %fusion.pick_ref), channel_id=1, source_target_pairs={{0,2},{2,0},{4,6},{6,4},{8,10},{10,8},{12,14},{14,12},{16,18},{18,... | collective-permute-start | bytes 4718600 | tf_op jit(solution)/shard_map/ppermute | solution.py:710
  43.2 19.2 %collective-permute-start.4 = (bf16[1,2,256,384]{3,2,1,0:T(8,128)(2,1)}, bf16[1,2,256,384]{3,2,1,0:T(8,128)(2,1)}, u32[]{:S(2)}, u32[]{:S(2)}) collective-permute-start(bf16[1,2,256,384]{3,2,1,0:T(8,128)(2,1)} %bitcast.refs_0_), channel_id=1, source_target_pairs={{0,16},{2,18},{4,20},{6,22},{8,24},{10,26},{12,28},{14,30},{16,0},... | collective-permute-start | bytes 1179656 | tf_op jit(solution)/shard_map/ppermute | solution.py:710
  45.8 18.4 %collective-permute-start.10 = (bf16[1,2,256,384]{3,2,1,0:T(8,128)(2,1)}, bf16[1,2,256,384]{3,2,1,0:T(8,128)(2,1)}, u32[]{:S(2)}, u32[]{:S(2)}) collective-permute-start(bf16[1,2,256,384]{3,2,1,0:T(8,128)(2,1)} %bitcast.refs_0_), channel_id=1, source_target_pairs={{0,8},{2,10},{4,12},{6,14},{8,0},{10,2},{12,4},{14,6},{16,24},{18,... | collective-permute-start | bytes 1179656 | tf_op jit(solution)/shard_map/ppermute | solution.py:710
  62.6 21.6 %collective-permute-start.12 = (bf16[1,2,256,384]{3,2,1,0:T(8,128)(2,1)}, bf16[1,2,256,384]{3,2,1,0:T(8,128)(2,1)}, u32[]{:S(2)}, u32[]{:S(2)}) collective-permute-start(bf16[1,2,256,384]{3,2,1,0:T(8,128)(2,1)} %bitcast.refs_0_), channel_id=1, source_target_pairs={{0,4},{2,6},{4,0},{6,2},{8,12},{10,14},{12,8},{14,10},{16,20},{18,... | collective-permute-start | bytes 1179656 | tf_op jit(solution)/shard_map/ppermute | solution.py:710
  64.2 23.9 %collective-permute-start.11 = (bf16[1,2,256,384]{3,2,1,0:T(8,128)(2,1)}, bf16[1,2,256,384]{3,2,1,0:T(8,128)(2,1)}, u32[]{:S(2)}, u32[]{:S(2)}) collective-permute-start(bf16[1,2,256,384]{3,2,1,0:T(8,128)(2,1)} %collective-permute-done.10.refs_0_), channel_id=1, source_target_pairs={{0,4},{2,6},{4,0},{6,2},{8,12},{10,14},{12,8},{14,10},{16,20},{18,... | collective-permute-start | bytes 1179656 | tf_op jit(solution)/shard_map/ppermute | solution.py:710
  64.7 27.3 %collective-permute-start.9 = (bf16[1,2,256,384]{3,2,1,0:T(8,128)(2,1)}, bf16[1,2,256,384]{3,2,1,0:T(8,128)(2,1)S(1)}, u32[]{:S(2)}, u32[]{:S(2)}) collective-permute-start(bf16[1,2,256,384]{3,2,1,0:T(8,128)(2,1)} %collective-permute-done.4.refs_0_), channel_id=1, source_target_pairs={{0,4},{2,6},{4,0},{6,2},{8,12},{10,14},{12,8},{14,10},{16,20},{18,... | collective-permute-start | bytes 1179656 | tf_op jit(solution)/shard_map/ppermute | solution.py:710
  73.0 25.9 %collective-permute-start.6 = (bf16[1,2,256,384]{3,2,1,0:T(8,128)(2,1)}, bf16[1,2,256,384]{3,2,1,0:T(8,128)(2,1)S(1)}, u32[]{:S(2)}, u32[]{:S(2)}) collective-permute-start(bf16[1,2,256,384]{3,2,1,0:T(8,128)(2,1)} %collective-permute-done.5.refs_0_), channel_id=1, source_target_pairs={{0,4},{2,6},{4,0},{6,2},{8,12},{10,14},{12,8},{14,10},{16,20},{18,... | collective-permute-start | bytes 1179656 | tf_op jit(solution)/shard_map/ppermute | solution.py:710
  134.3 17.7 %collective-permute-start.60 = (bf16[128,1536]{1,0:T(8,128)(2,1)S(1)}, bf16[128,1536]{1,0:T(8,128)(2,1)S(1)}, u32[]{:S(2)}, u32[]{:S(2)}) collective-permute-start(bf16[128,1536]{1,0:T(8,128)(2,1)S(1)} %get-tuple-element.219.refs_2_), channel_id=1, source_target_pairs={{0,2},{2,0},{4,6},{6,4},{8,10},{10,8},{12,14},{14,12},{16,18},{18,... | collective-permute-start | bytes 1179656 | tf_op jit(solution)/shard_map/ppermute | solution.py:710
  134.6 19.5 %collective-permute-start.62 = (bf16[128,1536]{1,0:T(8,128)(2,1)S(1)}, bf16[128,1536]{1,0:T(8,128)(2,1)S(1)}, u32[]{:S(2)}, u32[]{:S(2)}) collective-permute-start(bf16[128,1536]{1,0:T(8,128)(2,1)S(1)} %get-tuple-element.221.refs_6_), channel_id=1, source_target_pairs={{0,2},{2,0},{4,6},{6,4},{8,10},{10,8},{12,14},{14,12},{16,18},{18,... | collective-permute-start | bytes 1179656 | tf_op jit(solution)/shard_map/ppermute | solution.py:710
  139.8 17.0 %collective-permute-start.24 = (bf16[1,2,256,384]{3,2,1,0:T(8,128)(2,1)S(1)}, bf16[1,2,256,384]{3,2,1,0:T(8,128)(2,1)S(1)}, u32[]{:S(2)}, u32[]{:S(2)}) collective-permute-start(bf16[1,2,256,384]{3,2,1,0:T(8,128)(2,1)S(1)} %get-tuple-element.171), channel_id=1, source_target_pairs={{0,4},{2,6},{4,0},{6,2},{8,12},{10,14},{12,8},{14,10},{16,20},{18,... | collective-permute-start | bytes 1179656 | tf_op jit(solution)/shard_map/ppermute | solution.py:710
  152.6 19.9 %collective-permute-start.23 = (bf16[1,2,256,384]{3,2,1,0:T(8,128)(2,1)S(1)}, bf16[1,2,256,384]{3,2,1,0:T(8,128)(2,1)S(1)}, u32[]{:S(2)}, u32[]{:S(2)}) collective-permute-start(bf16[1,2,256,384]{3,2,1,0:T(8,128)(2,1)S(1)} %get-tuple-element.169), channel_id=1, source_target_pairs={{0,4},{2,6},{4,0},{6,2},{8,12},{10,14},{12,8},{14,10},{16,20},{18,... | collective-permute-start | bytes 1179656 | tf_op jit(solution)/shard_map/ppermute | solution.py:710
  156.3 53.9 %collective-permute-start.65 = (bf16[192,3456]{1,0:T(8,128)(2,1)S(1)}, bf16[192,3456]{1,0:T(8,128)(2,1)}, u32[]{:S(2)}, u32[]{:S(2)}) collective-permute-start(bf16[192,3456]{1,0:T(8,128)(2,1)S(1)} %get-tuple-element.225), channel_id=1, source_target_pairs={{0,4},{2,6},{4,0},{6,2},{8,12},{10,14},{12,8},{14,10},{16,20},{18,... | collective-permute-start | bytes 3981320 | tf_op jit(solution)/shard_map/ppermute | solution.py:710
  157.0 15.8 %collective-permute-start.25 = (bf16[1,2,256,384]{3,2,1,0:T(8,128)(2,1)S(1)}, bf16[1,2,256,384]{3,2,1,0:T(8,128)(2,1)S(1)}, u32[]{:S(2)}, u32[]{:S(2)}) collective-permute-start(bf16[1,2,256,384]{3,2,1,0:T(8,128)(2,1)S(1)} %add_convert_fusion.1), channel_id=1, source_target_pairs={{0,8},{2,10},{4,12},{6,14},{8,0},{10,2},{12,4},{14,6},{16,24},{18,... | collective-permute-start | bytes 1179656 | tf_op jit(solution)/shard_map/ppermute | solution.py:710
  163.9 44.5 %collective-permute-start.20 = (bf16[1,2,256,384]{3,2,1,0:T(8,128)(2,1)S(1)}, bf16[1,2,256,384]{3,2,1,0:T(8,128)(2,1)S(1)}, u32[]{:S(2)}, u32[]{:S(2)}) collective-permute-start(bf16[1,2,256,384]{3,2,1,0:T(8,128)(2,1)S(1)} %get-tuple-element.165), channel_id=1, source_target_pairs={{0,4},{2,6},{4,0},{6,2},{8,12},{10,14},{12,8},{14,10},{16,20},{18,... | collective-permute-start | bytes 1179656 | tf_op jit(solution)/shard_map/ppermute | solution.py:710
  172.5 36.0 %collective-permute-start.22 = (bf16[1,2,256,384]{3,2,1,0:T(8,128)(2,1)S(1)}, bf16[1,2,256,384]{3,2,1,0:T(8,128)(2,1)S(1)}, u32[]{:S(2)}, u32[]{:S(2)}) collective-permute-start(bf16[1,2,256,384]{3,2,1,0:T(8,128)(2,1)S(1)} %add_convert_fusion.2), channel_id=1, source_target_pairs={{0,8},{2,10},{4,12},{6,14},{8,0},{10,2},{12,4},{14,6},{16,24},{18,... | collective-permute-start | bytes 1179656 | tf_op jit(solution)/shard_map/ppermute | solution.py:710
  172.9 36.0 %collective-permute-start.26 = (bf16[1,2,256,384]{3,2,1,0:T(8,128)(2,1)S(1)}, bf16[1,2,256,384]{3,2,1,0:T(8,128)(2,1)S(1)}, u32[]{:S(2)}, u32[]{:S(2)}) collective-permute-start(bf16[1,2,256,384]{3,2,1,0:T(8,128)(2,1)S(1)} %add_convert_fusion), channel_id=1, source_target_pairs={{0,16},{2,18},{4,20},{6,22},{8,24},{10,26},{12,28},{14,30},{16,0},... | collective-permute-start | bytes 1179656 | tf_op jit(solution)/shard_map/ppermute | solution.py:710
  182.9 46.4 %collective-permute-start.50 = (bf16[128,768]{1,0:T(8,128)(2,1)S(1)}, bf16[128,768]{1,0:T(8,128)(2,1)S(1)}, u32[]{:S(2)}, u32[]{:S(2)}) collective-permute-start(bf16[128,768]{1,0:T(8,128)(2,1)S(1)} %copy-done.15), channel_id=1, source_target_pairs={{0,2},{2,0},{4,6},{6,4},{8,10},{10,8},{12,14},{14,12},{16,18},{18,... | collective-permute-start | bytes 589832 | tf_op jit(solution)/shard_map/ppermute | solution.py:710
  208.5 19.3 %collective-permute-start.53 = (bf16[128,384]{1,0:T(8,128)(2,1)S(1)}, bf16[128,384]{1,0:T(8,128)(2,1)S(1)}, u32[]{:S(2)}, u32[]{:S(2)}) collective-permute-start(bf16[128,384]{1,0:T(8,128)(2,1)S(1)} %get-tuple-element.213.refs_10_), channel_id=1, source_target_pairs={{0,2},{2,0},{4,6},{6,4},{8,10},{10,8},{12,14},{14,12},{16,18},{18,... | collective-permute-start | bytes 294920 | tf_op jit(solution)/shard_map/ppermute | solution.py:710
  208.5 20.9 %collective-permute-start.48 = (bf16[128,768]{1,0:T(8,128)(2,1)S(1)}, bf16[128,768]{1,0:T(8,128)(2,1)S(1)}, u32[]{:S(2)}, u32[]{:S(2)}) collective-permute-start(bf16[128,768]{1,0:T(8,128)(2,1)S(1)} %get-tuple-element.209.refs_0_), channel_id=1, source_target_pairs={{0,2},{2,0},{4,6},{6,4},{8,10},{10,8},{12,14},{14,12},{16,18},{18,... | collective-permute-start | bytes 589832 | tf_op jit(solution)/shard_map/ppermute | solution.py:710
  209.0 20.8 %collective-permute-start.54 = (bf16[256,768]{1,0:T(8,128)(2,1)S(1)}, bf16[256,768]{1,0:T(8,128)(2,1)S(1)}, u32[]{:S(2)}, u32[]{:S(2)}) collective-permute-start(bf16[256,768]{1,0:T(8,128)(2,1)S(1)} %copy-done.46), channel_id=1, source_target_pairs={{0,2},{2,0},{4,6},{6,4},{8,10},{10,8},{12,14},{14,12},{16,18},{18,... | collective-permute-start | bytes 1179656 | tf_op jit(solution)/shard_map/ppermute | solution.py:710
  229.3 17.5 %collective-permute-start.55 = (bf16[256,768]{1,0:T(8,128)(2,1)}, bf16[256,768]{1,0:T(8,128)(2,1)}, u32[]{:S(2)}, u32[]{:S(2)}) collective-permute-start(bf16[256,768]{1,0:T(8,128)(2,1)} %get-tuple-element.215.refs_14_), channel_id=1, source_target_pairs={{0,2},{2,0},{4,6},{6,4},{8,10},{10,8},{12,14},{14,12},{16,18},{18,... | collective-permute-start | bytes 1179656 | tf_op jit(solution)/shard_map/ppermute | solution.py:710
  229.4 28.8 %collective-permute-start.66 = (bf16[2,1,48,3456]{3,2,1,0:T(8,128)(2,1)}, bf16[2,1,48,3456]{3,2,1,0:T(8,128)(2,1)}, u32[]{:S(2)}, u32[]{:S(2)}) collective-permute-start(bf16[2,1,48,3456]{3,2,1,0:T(8,128)(2,1)} %pad_maximum_fusion), channel_id=1, source_target_pairs={{0,8},{2,10},{4,12},{6,14},{8,0},{10,2},{12,4},{14,6},{16,24},{18,... | collective-permute-start | bytes 1990664 | tf_op jit(solution)/shard_map/ppermute | solution.py:710
  229.8 16.6 %collective-permute-start.51 = (bf16[128,1152]{1,0:T(8,128)(2,1)}, bf16[128,1152]{1,0:T(8,128)(2,1)S(1)}, u32[]{:S(2)}, u32[]{:S(2)}) collective-permute-start(bf16[128,1152]{1,0:T(8,128)(2,1)} %get-tuple-element.211.refs_6_), channel_id=1, source_target_pairs={{0,2},{2,0},{4,6},{6,4},{8,10},{10,8},{12,14},{14,12},{16,18},{18,... | collective-permute-start | bytes 884744 | tf_op jit(solution)/shard_map/ppermute | solution.py:710
  230.0 16.3 %collective-permute-start.52 = (bf16[128,768]{1,0:T(8,128)(2,1)}, bf16[128,768]{1,0:T(8,128)(2,1)}, u32[]{:S(2)}, u32[]{:S(2)}) collective-permute-start(bf16[128,768]{1,0:T(8,128)(2,1)} %get-tuple-element.212.refs_8_), channel_id=1, source_target_pairs={{0,2},{2,0},{4,6},{6,4},{8,10},{10,8},{12,14},{14,12},{16,18},{18,... | collective-permute-start | bytes 589832 | tf_op jit(solution)/shard_map/ppermute | solution.py:710
  260.8 30.2 %collective-permute-start.33 = (bf16[256,768]{1,0:T(8,128)(2,1)S(1)}, bf16[256,768]{1,0:T(8,128)(2,1)S(1)}, u32[]{:S(2)}, u32[]{:S(2)}) collective-permute-start(bf16[256,768]{1,0:T(8,128)(2,1)S(1)} %copy-done.18), channel_id=1, source_target_pairs={{0,2},{2,0},{4,6},{6,4},{8,10},{10,8},{12,14},{14,12},{16,18},{18,... | collective-permute-start | bytes 1179656 | tf_op jit(solution)/shard_map/ppermute | solution.py:710
  260.8 28.9 %collective-permute-start.36 = (bf16[256,384]{1,0:T(8,128)(2,1)S(1)}, bf16[256,384]{1,0:T(8,128)(2,1)S(1)}, u32[]{:S(2)}, u32[]{:S(2)}) collective-permute-start(bf16[256,384]{1,0:T(8,128)(2,1)S(1)} %copy-done.52), channel_id=1, source_target_pairs={{0,2},{2,0},{4,6},{6,4},{8,10},{10,8},{12,14},{14,12},{16,18},{18,... | collective-permute-start | bytes 589832 | tf_op jit(solution)/shard_map/ppermute | solution.py:710
  261.3 24.9 %collective-permute-start.56 = (bf16[192,2688]{1,0:T(8,128)(2,1)S(1)}, bf16[192,2688]{1,0:T(8,128)(2,1)}, u32[]{:S(2)}, u32[]{:S(2)}) collective-permute-start(bf16[192,2688]{1,0:T(8,128)(2,1)S(1)} %get-tuple-element.217), channel_id=1, source_target_pairs={{0,4},{2,6},{4,0},{6,2},{8,12},{10,14},{12,8},{14,10},{16,20},{18,... | collective-permute-start | bytes 3096584 | tf_op jit(solution)/shard_map/ppermute | solution.py:710
  261.8 18.4 %collective-permute-start.67 = (bf16[1,48,3456]{2,1,0:T(8,128)(2,1)}, bf16[1,48,3456]{2,1,0:T(8,128)(2,1)}, u32[]{:S(2)}, u32[]{:S(2)}) collective-permute-start(bf16[1,48,3456]{2,1,0:T(8,128)(2,1)} %fusion.23), channel_id=1, source_target_pairs={{0,16},{2,18},{4,20},{6,22},{8,24},{10,26},{12,28},{14,30},{16,0},... | collective-permute-start | bytes 995336 | tf_op jit(solution)/shard_map/ppermute | solution.py:710
  269.3 21.6 %collective-permute-start.34 = (bf16[256,1152]{1,0:T(8,128)(2,1)S(1)}, bf16[256,1152]{1,0:T(8,128)(2,1)S(1)}, u32[]{:S(2)}, u32[]{:S(2)}) collective-permute-start(bf16[256,1152]{1,0:T(8,128)(2,1)S(1)} %copy-done.28), channel_id=1, source_target_pairs={{0,2},{2,0},{4,6},{6,4},{8,10},{10,8},{12,14},{14,12},{16,18},{18,... | collective-permute-start | bytes 1769480 | tf_op jit(solution)/shard_map/ppermute | solution.py:710
  289.7 52.0 %collective-permute-start.45 = (bf16[192,3072]{1,0:T(8,128)(2,1)S(1)}, bf16[192,3072]{1,0:T(8,128)(2,1)S(1)}, u32[]{:S(2)}, u32[]{:S(2)}) collective-permute-start(bf16[192,3072]{1,0:T(8,128)(2,1)S(1)} %copy-done.87), channel_id=1, source_target_pairs={{0,4},{2,6},{4,0},{6,2},{8,12},{10,14},{12,8},{14,10},{16,20},{18,... | collective-permute-start | bytes 3538952 | tf_op jit(solution)/shard_map/ppermute | solution.py:710
  293.2 37.0 %collective-permute-start.38 = (bf16[192,1664]{1,0:T(8,128)(2,1)S(1)}, bf16[192,1664]{1,0:T(8,128)(2,1)S(1)}, u32[]{:S(2)}, u32[]{:S(2)}) collective-permute-start(bf16[192,1664]{1,0:T(8,128)(2,1)S(1)} %get-tuple-element.202), channel_id=1, source_target_pairs={{0,4},{2,6},{4,0},{6,2},{8,12},{10,14},{12,8},{14,10},{16,20},{18,... | collective-permute-start | bytes 1916936 | tf_op jit(solution)/shard_map/ppermute | solution.py:710
  300.9 31.4 %collective-permute-start.58 = (bf16[1,48,2688]{2,1,0:T(8,128)(2,1)S(1)}, bf16[1,48,2688]{2,1,0:T(8,128)(2,1)S(1)}, u32[]{:S(2)}, u32[]{:S(2)}) collective-permute-start(bf16[1,48,2688]{2,1,0:T(8,128)(2,1)S(1)} %fusion.31), channel_id=1, source_target_pairs={{0,16},{2,18},{4,20},{6,22},{8,24},{10,26},{12,28},{14,30},{16,0},... | collective-permute-start | bytes 774152 | tf_op jit(solution)/shard_map/ppermute | solution.py:710
  (127 other events, 1414.8 us)
